TPU v7x, 32 devices: a whole 2x2x4 slice. The times are simulated.
32 devices in a mesh: rep: 4 (over x, core), dp: 8 (over z, y).
Axes of the slice: x: 2, y: 2, z: 4, core: 2. Of those that a mesh axis runs over, the one named last changes fastest.
Arguments:
- images: bfloat16 [1024, 7, 7, 2048], P(('rep', 'dp'))
- labels: int32 [1024], P(('rep', 'dp')), may hold values from 0 to 999
- conv_weight: float32 [13, 512, 512], P(None, 'dp'), may hold values from -0.1875 to 0.1875
- conv_mask: int32 [13, 512, 512], P(None, 'dp'), may hold values 0 or 1
- conv_rank: int32 [13, 512, 512], P(None, 'dp'), may hold values from 0 to 262143, as said below
- head_weight: float32 [512, 1000], P('dp'), may hold values from -0.25 to 0.25
- norm_params: float32 [4, 512], replicated, may hold values from 0.5 to 1.5
- head_bias: float32 [1000], replicated, may hold values from -3 to 3
- conv_first: float32 [4, 13, 512, 512], P('rep', None, 'dp'), may hold values from -0.000125 to 0.000125
- conv_second: float32 [4, 13, 512, 512], P('rep', None, 'dp'), may hold values from 1.7578125e-11 to 2.8125e-10
- head_first: float32 [4, 512, 1000], P('rep', 'dp'), may hold values from -0.0004125 to 0.0004125
- head_second: float32 [4, 512, 1000], P('rep', 'dp'), may hold values from 1.953125e-10 to 3.125e-09
- norm_first: float32 [4, 4, 512], P('rep'), may hold values from -0.00020625 to 0.00020625
- norm_second: float32 [4, 4, 512], P('rep'), may hold values from 4.8828126e-11 to 7.8125e-10
- bias_first: float32 [4, 1000], P('rep'), may hold values from -0.00125 to 0.00125
- bias_second: float32 [4, 1000], P('rep'), may hold values from 1.7578125e-09 to 2.8125e-08
- conv_outer: float32 [13, 512, 512], P(None, 'dp'), may hold values from -0.12 to 0.12
- head_outer: float32 [512, 1000], P('dp'), may hold values from -0.12 to 0.12
- norm_outer: float32 [4, 512], replicated, may hold values from -0.12 to 0.12
- bias_outer: float32 [1000], replicated, may hold values from -0.12 to 0.12
Outputs:
- conv_weight_new: float32 [13, 512, 512], P(None, 'dp')
- conv_mask_new: int32 [13, 512, 512], P(None, 'dp')
- conv_first_new: float32 [4, 13, 512, 512], P('rep', None, 'dp')
- conv_second_new: float32 [4, 13, 512, 512], P('rep', None, 'dp')
- conv_outer_new: float32 [13, 512, 512], P(None, 'dp')
- head_weight_new: float32 [512, 1000], P('dp')
- head_first_new: float32 [4, 512, 1000], P('rep', 'dp')
- head_second_new: float32 [4, 512, 1000], P('rep', 'dp')
- head_outer_new: float32 [512, 1000], P('dp')
- norm_new: float32 [4, 512], replicated
- norm_first_new: float32 [4, 4, 512], P('rep')
- norm_second_new: float32 [4, 4, 512], P('rep')
- norm_outer_new: float32 [4, 512], replicated
- bias_new: float32 [1000], replicated
- bias_first_new: float32 [4, 1000], P('rep')
- bias_second_new: float32 [4, 1000], P('rep')
- bias_outer_new: float32 [1000], replicated
- loss_sums: float32 [4], P('rep')
Inputs may be any that keep to these rules, and one draw needn't show every extreme that they name: `conv_rank`: each block of 512 x 512 entries holds each number of 0 to 262143 once.
All inputs are finite; a program needn't handle non-finite values. No bound on the sum of `conv_mask` on one device may be relied on, other than what follows from the above.
Results may differ from a plain program's by a relative error of at most 0.01065.
The roundings to bfloat16 on the way count: a program that leaves them out, or rounds other values in their place, can miss the bound.
Values may be sent and summed in bfloat16 or wider, within the bound.
No kernel may reach another device: no remote copies, remote signals or barrier semaphores. Data moves between devices by JAX's collectives and lax.ppermute only.
A program may use at most 256 MiB of HBM per device.

v0:
```python
import jax
import jax.numpy as jnp
from jax import lax
from jax.sharding import PartitionSpec as P

C_IN = 2048
C_MID = 512
CLASSES = 1000
SIDE = 7
STEP = 10
PIX = 49
DROP_CUT = 78643
GROW_CUT = 242484


def unfold(maps):
    padded = jnp.pad(maps, ((0, 0), (1, 1), (1, 1), (0, 0)))
    pieces = [padded[:, a : a + SIDE, b : b + SIDE, :] for a in range(3) for b in range(3)]
    return jnp.concatenate(pieces, axis=-1).reshape(maps.shape[0] * PIX, 9 * maps.shape[3])


def fold_back(grads, batch):
    width = grads.shape[1] // 9
    shaped = grads.reshape(batch, SIDE, SIDE, 9, width)
    total = jnp.zeros((batch, SIDE + 2, SIDE + 2, width), jnp.float32)
    for a in range(3):
        for b in range(3):
            total = total + jnp.pad(
                shaped[:, :, :, 3 * a + b, :], ((0, 0), (a, 2 - a), (b, 2 - b), (0, 0))
            )
    return total[:, 1 : SIDE + 1, 1 : SIDE + 1, :].reshape(batch * PIX, width)


def norm_forward(pre, gain, shift, total):
    sums, squares = lax.psum((jnp.sum(pre, axis=0), jnp.sum(pre * pre, axis=0)), "dp")
    mean = sums / total
    var = squares / total - mean * mean
    rstd = lax.rsqrt(var + 1e-05)
    normed = (pre - mean) * rstd
    shifted = gain * normed + shift
    return (jax.nn.silu(shifted), (normed, shifted, rstd))


def norm_backward(grad_out, saved, gain, total, extra_one, extra_two):
    normed, shifted, rstd = saved
    sig = jax.nn.sigmoid(shifted)
    grad_pre = grad_out * sig * (1.0 + shifted * (1.0 - sig))
    gain_sum, shift_sum, one_sum, two_sum = lax.psum(
        (jnp.sum(grad_pre * normed, axis=0), jnp.sum(grad_pre, axis=0), extra_one, extra_two), "dp"
    )
    grad_in = gain * rstd * (grad_pre - shift_sum / total - normed * gain_sum / total)
    return (grad_in.astype(jnp.bfloat16), gain_sum, shift_sum, one_sum, two_sum)


def adamw(weight, grad, first, second, rate):
    first = 0.9 * first + 0.1 * grad
    second = 0.999 * second + 0.001 * grad * grad
    normal_step = first / (1.0 - 0.9**STEP) / (jnp.sqrt(second / (1.0 - 0.999**STEP)) + 1e-08)
    return (weight - rate * (normal_step + 0.01 * weight), first, second)


def outer_step(start, group_sum, momentum, groups):
    delta = start - group_sum / groups
    momentum = 0.9 * momentum + delta
    return (start - 0.7 * (delta + 0.9 * momentum), momentum)


def per_device(
    images,
    labels,
    conv_weight,
    conv_mask,
    conv_rank,
    head_weight,
    norm_params,
    head_bias,
    conv_first,
    conv_second,
    head_first,
    head_second,
    norm_first,
    norm_second,
    bias_first,
    bias_second,
    conv_outer,
    head_outer,
    norm_outer,
    bias_outer,
):
    devices = lax.axis_size("dp")
    groups = lax.axis_size("rep")
    width = C_MID
    blocks = C_IN // C_MID
    mask_old = conv_mask.astype(jnp.float32)
    dropped = (conv_mask == 1) & (conv_rank < DROP_CUT)
    grown = (conv_mask == 0) & (conv_rank >= GROW_CUT)
    mask_int = jnp.where(dropped, 0, jnp.where(grown, 1, conv_mask))
    mask_new = mask_int.astype(jnp.float32)
    kept = mask_old * mask_new
    effective = conv_weight * mask_old
    start = conv_weight * kept
    conv_full, head_full = (
        lax.all_gather(effective.astype(jnp.bfloat16), "dp", axis=1, tiled=True),
        lax.all_gather(head_weight.astype(jnp.bfloat16), "dp", axis=0, tiled=True),
    )
    first_conv = conv_full[:blocks].reshape(C_IN, width)
    taps = conv_full[blocks:].reshape(9 * width, width)
    batch = images.shape[0]
    rows = batch * PIX
    total = rows * devices
    group_images = batch * devices
    inputs = images.reshape(rows, C_IN)
    y_one = jnp.dot(inputs, first_conv, preferred_element_type=jnp.float32)
    h_one, saved_one = norm_forward(y_one, norm_params[0], norm_params[1], total)
    patches = unfold(h_one.astype(jnp.bfloat16).reshape(batch, SIDE, SIDE, width))
    y_two = jnp.dot(patches, taps, preferred_element_type=jnp.float32)
    h_two, saved_two = norm_forward(y_two, norm_params[2], norm_params[3], total)
    pooled = jnp.mean(h_two.reshape(batch, PIX, width), axis=1).astype(jnp.bfloat16)
    logits = jnp.dot(pooled, head_full, preferred_element_type=jnp.float32) + head_bias
    onehot = (labels[:, None] == jnp.arange(CLASSES, dtype=jnp.int32)[None, :]).astype(jnp.float32)
    top = jnp.max(logits, axis=1, keepdims=True)
    expsum = jnp.sum(jnp.exp(logits - top), axis=1, keepdims=True)
    lse = top + jnp.log(expsum)
    loss_local = jnp.sum(lse[:, 0] - jnp.sum(logits * onehot, axis=1))
    dlogits = ((jnp.exp(logits - lse) - onehot) / group_images).astype(jnp.bfloat16)
    head_grad_local = jnp.dot(pooled.T, dlogits, preferred_element_type=jnp.float32)
    bias_local = jnp.sum(dlogits.astype(jnp.float32), axis=0)
    dpool = jnp.dot(dlogits, head_full.T, preferred_element_type=jnp.float32) / PIX
    dh_two = jnp.broadcast_to(dpool[:, None, :], (batch, PIX, width)).reshape(rows, width)
    dy_two, gain_two, shift_two, bias_grad, loss_sum = norm_backward(
        dh_two, saved_two, norm_params[2], total, bias_local, loss_local.reshape(1)
    )
    taps_grad = jnp.dot(patches.T, dy_two, preferred_element_type=jnp.float32)
    dpatches = jnp.dot(dy_two, taps.T, preferred_element_type=jnp.float32)
    dh_one = fold_back(dpatches, batch)
    empty = jnp.zeros((0,), jnp.float32)
    dy_one, gain_one, shift_one, unused_one, unused_two = norm_backward(
        dh_one, saved_one, norm_params[0], total, empty, empty
    )
    first_grad = jnp.dot(inputs.T, dy_one, preferred_element_type=jnp.float32)
    first_owned, taps_owned, head_grad = (
        lax.psum_scatter(
            first_grad.reshape(blocks, width, width), "dp", scatter_dimension=1, tiled=True
        ),
        lax.psum_scatter(taps_grad.reshape(9, width, width), "dp", scatter_dimension=1, tiled=True),
        lax.psum_scatter(head_grad_local, "dp", scatter_dimension=0, tiled=True),
    )
    dense = jnp.concatenate([first_owned, taps_owned], axis=0) + 5e-05 * effective
    norm_grad = jnp.stack([gain_one, shift_one, gain_two, shift_two])
    conv_g, conv_m, conv_v = adamw(
        start, mask_new * dense, conv_first[0] * kept, conv_second[0] * kept, 0.03
    )
    conv_g = conv_g * mask_new
    head_g, head_m, head_v = adamw(head_weight, head_grad, head_first[0], head_second[0], 0.03)
    norm_g, norm_m, norm_v = adamw(norm_params, norm_grad, norm_first[0], norm_second[0], 0.3)
    bias_g, bias_m, bias_v = adamw(head_bias, bias_grad, bias_first[0], bias_second[0], 0.3)
    conv_sum, head_sum, norm_sum, bias_sum = lax.psum((conv_g, head_g, norm_g, bias_g), "rep")
    conv_new, conv_mom = outer_step(start, conv_sum, conv_outer, groups)
    head_new, head_mom = outer_step(head_weight, head_sum, head_outer, groups)
    norm_new, norm_mom = outer_step(norm_params, norm_sum, norm_outer, groups)
    bias_new, bias_mom = outer_step(head_bias, bias_sum, bias_outer, groups)
    return (
        conv_new * mask_new,
        mask_int,
        (conv_m * mask_new)[None],
        (conv_v * mask_new)[None],
        conv_mom * mask_new,
        head_new,
        head_m[None],
        head_v[None],
        head_mom,
        norm_new,
        norm_m[None],
        norm_v[None],
        norm_mom,
        bias_new,
        bias_m[None],
        bias_v[None],
        bias_mom,
        loss_sum,
    )


def solution(mesh):
    in_specs = (
        P(("rep", "dp"), None, None, None),
        P(("rep", "dp")),
        P(None, "dp", None),
        P(None, "dp", None),
        P(None, "dp", None),
        P("dp", None),
        P(),
        P(),
        P("rep", None, "dp", None),
        P("rep", None, "dp", None),
        P("rep", "dp", None),
        P("rep", "dp", None),
        P("rep", None, None),
        P("rep", None, None),
        P("rep", None),
        P("rep", None),
        P(None, "dp", None),
        P("dp", None),
        P(),
        P(),
    )
    out_specs = (
        P(None, "dp", None),
        P(None, "dp", None),
        P("rep", None, "dp", None),
        P("rep", None, "dp", None),
        P(None, "dp", None),
        P("dp", None),
        P("rep", "dp", None),
        P("rep", "dp", None),
        P("dp", None),
        P(),
        P("rep", None, None),
        P("rep", None, None),
        P(),
        P(),
        P("rep", None),
        P("rep", None),
        P(),
        P("rep"),
    )
    return jax.shard_map(
        per_device, mesh=mesh, in_specs=in_specs, out_specs=out_specs, check_vma=False
    )
```

profile of v0, /device:TPU:0, one launch (start us, length us, event | category | flops | bytes accessed | tf_op | source)
XLA Modules:
  0.0 733.8 jit_solution(12460823453539084988)
XLA Ops:
  10.6 9.4 %copy.50 = bf16[32,7,7,2048]{3,2,1,0:T(8,128)(2,1)} copy(bf16[32,7,7,2048]{3,0,2,1:T(8,128)(2,1)} %param.20) | data formatting | bytes 12845056 | tf_op args[0]
  20.0 9.6 %reshape.284 = bf16[1568,2048]{1,0:T(8,128)(2,1)} reshape(bf16[32,7,7,2048]{3,2,1,0:T(8,128)(2,1)} %copy.50) | data formatting | bytes 12845056 | tf_op jit(solution)/shard_map/reshape | solution.py:112
  29.7 39.8 %all_gather.7 = bf16[512,1000]{1,0:T(8,128)(2,1)} all-gather(bf16[64,1000]{1,0:T(8,128)(2,1)S(1)} %convert_element_type.58), channel_id=1, replica_groups=mesh['rep'=4,'dp'=8] {'dp'}, dimensions={0}, use_global_device_ids=true | all-gather | bytes 1152000 | tf_op jit(solution)/shard_map/all_gather | solution.py:104
  69.5 57.3 %all-gather.2.cloned.1.call-done = bf16[13,512,512]{2,1,0:T(8,128)(2,1)} async-done(((bf16[13,64,512]{2,1,0:T(8,128)(2,1)}), bf16[13,512,512]{2,1,0:T(8,128)(2,1)}) %all-gather.2.cloned.1.call-update) | async-done | bytes 6815760 | tf_op jit(solution)/shard_map/all_gather | solution.py:103
  128.4 5.6 fusion.47
  134.0 19.1 %all-reduce.13 = (f32[512]{0:T(512)S(1)}, f32[512]{0:T(512)S(1)}) all-reduce(f32[512]{0:T(512)S(1)} %get-tuple-element.25, f32[512]{0:T(512)S(1)} %get-tuple-element.24), channel_id=1, replica_groups=mesh['rep'=4,'dp'=8] {'dp'}, use_global_device_ids=true, to_apply=%region_1.2 | all-reduce | flops 1024 | bytes 8192 | tf_op jit(solution)/shard_map/psum | solution.py:35
  159.5 11.7 %pad_slice_fusion = (bf16[32,7,7,512]{3,2,1,0:T(8,128)(2,1)}, bf16[32,7,7,512]{3,2,1,0:T(8,128)(2,1)}, bf16[32,7,7,512]{3,2,1,0:T(8,128)(2,1)}, bf16[32,7,7,512]...) fusion(bf16[32,7,7,512]{3,2,1,0:T(8,128)(2,1)} %reshape.285), kind=kLoop, calls=%fused_computation | loop fusion | bytes 14450688 | tf_op jit(solution)/shard_map/slice | solution.py:18
  220.4 12.0 %fusion.46 = (f32[512]{0:T(512)S(1)}, f32[512]{0:T(512)S(1)}, f32[1568,512]{1,0:T(8,128)}) fusion(bf16[1568,4608]{1,0:T(8,128)(2,1)} %constant_dynamic-update-slice_fusion, bf16[4608,512]{1,0:T(8,128)(2,1)S(1)} %bitcast.157), kind=kOutput, calls=%fused_computation.148 | convolution fusion | flops 7401159680 | bytes 22384640 | tf_op jit(solution)/shard_map/dot_general | solution.py:116
  232.5 17.6 %all-reduce.12 = (f32[512]{0:T(512)S(1)}, f32[512]{0:T(512)S(1)}) all-reduce(f32[512]{0:T(512)S(1)} %get-tuple-element.23, f32[512]{0:T(512)S(1)} %get-tuple-element.22), channel_id=1, replica_groups=mesh['rep'=4,'dp'=8] {'dp'}, use_global_device_ids=true, to_apply=%region_5.6 | all-reduce | flops 1024 | bytes 8192 | tf_op jit(solution)/shard_map/psum | solution.py:35
  250.6 4.6 fusion.8
  276.6 6.3 fusion.45
  282.9 18.9 %all-reduce.11 = (f32[512]{0:T(512)S(1)}, f32[512]{0:T(512)S(1)}) all-reduce(f32[512]{0:T(512)S(1)} %get-tuple-element.21, f32[512]{0:T(512)S(1)} %get-tuple-element.20), channel_id=1, replica_groups=mesh['rep'=4,'dp'=8] {'dp'}, use_global_device_ids=true, to_apply=%region_14.15 | all-reduce | flops 1024 | bytes 8192 | tf_op jit(solution)/shard_map/psum | solution.py:48
  301.7 4.9 multiply_convert_fusion
  310.8 16.1 %fusion = f32[32,7,7,9,512]{4,0,3,2,1:T(8,128)} fusion(bf16[32,7,7,512,1]{3,2,1,0,4:T(8,128)(2,1)} %bitcast.158, bf16[13,512,512]{2,1,0:T(8,128)(2,1)} %all-gather.2.cloned.1.call-done), kind=kOutput, calls=%fused_computation.9 | convolution fusion | flops 7398752256 | bytes 35454976 | tf_op jit(solution)/shard_map/dot_general | solution.py:134
  326.9 18.4 %slice_bitcast_fusion.8 = (f32[32,7,7,512]{3,0,2,1:T(8,128)}, f32[32,7,7,512]{3,0,2,1:T(8,128)}, f32[32,7,7,512]{3,0,2,1:T(8,128)}, f32[32,7,7,512]{3,0,2,1:T(8,...) fusion(f32[32,7,7,9,512]{4,0,3,2,1:T(8,128)} %fusion), kind=kLoop, calls=%fused_computation.26 | loop fusion | bytes 57802752 | tf_op jit(solution)/shard_map/squeeze | solution.py:29
  345.4 5.4 pad_add_fusion
  353.0 4.2 pad_add_fusion.1
  357.2 3.8 copy.60
  361.0 4.7 reshape.289
  365.7 5.3 fusion.44
  371.0 18.8 %all-reduce.10 = (f32[512]{0:T(512)S(1)}, f32[512]{0:T(512)S(1)}, f32[1000]{0:T(1024)S(1)}, f32[1]{0:T(128)}) all-reduce(f32[512]{0:T(512)S(1)} %get-tuple-element.19, f32[512]{0:T(512)S(1)} %get-tuple-element.18, f32[1000]{0:T(1024)S(1)} %copy-done.36, f32[1]{0:T(128)} %bitcast.46), channel_id=1, replica_groups=mesh['rep'=4,'dp'=8] {'dp'}, use_global_device_ids=true, to_apply=%region_18.19 | all-reduce | flops 2025 | bytes 16200 | tf_op jit(solution)/shard_map/psum | solution.py:48
  389.8 10.0 %convolution_bitcast_fusion = f32[2048,512]{0,1:T(8,128)} fusion(bf16[1568,2048]{1,0:T(8,128)(2,1)} %reshape.284, f32[1568,512]{1,0:T(8,128)} %get-tuple-element.57, f32[512,1568]{0,1:T(8,128)S(1)} %get-tuple-element.95, f32[512]{0:T(512)S(1)} %get-tuple-element.28, f32[512]{0:T(512)S(1)} %broadcast_multiply_fusion.2, f32[512]{0:T(512)S(1)} %get-tuple-element.90, ...), kind=kOutput, calls=%fused_computation.11 | convolution fusion | flops 3294756864 | bytes 17049600 | tf_op jit(solution)/shard_map/dot_general | solution.py:140
  399.8 5.4 copy.61
  405.3 19.4 %copy.62 = bf16[4608,1568]{1,0:T(8,128)(2,1)} copy(bf16[4608,1568]{0,1:T(8,128)(2,1)} %bitcast.153) | data formatting | bytes 28901376 | tf_op jit(solution)/shard_map/dot_general | solution.py:133
  424.7 14.2 %fusion.15 = f32[9,512,512]{2,1,0:T(8,128)} fusion(bf16[9,512,1568]{2,1,0:T(8,128)(2,1)} %bitcast.155, bf16[1568,512]{1,0:T(8,128)(2,1)S(1)} %copy-done.11), kind=kOutput, calls=%fused_computation.68 | convolution fusion | flops 7398752256 | bytes 25493504 | tf_op jit(solution)/shard_map/dot_general | solution.py:133
  442.0 50.0 %reduce-scatter.4.cloned.1.call-done = f32[4,64,512]{2,1,0:T(8,128)} async-done(((f32[4,512,512]{2,1,0:T(8,128)}), f32[4,64,512]{2,1,0:T(8,128)}) %reduce-scatter.4.cloned.1.call-update) | async-done | bytes 524304 | tf_op jit(solution)/shard_map/reduce_scatter | solution.py:142
  492.0 167.5 %reduce-scatter.6.cloned.1.call-done = f32[9,64,512]{2,1,0:T(8,128)} async-done(((f32[9,512,512]{2,1,0:T(8,128)}), f32[9,64,512]{2,1,0:T(8,128)}) %reduce-scatter.6.cloned.1.call-update) | async-done | bytes 1179664 | tf_op jit(solution)/shard_map/reduce_scatter | solution.py:145
  659.5 5.5 multiply_bitcast_fusion
  665.1 6.3 multiply_bitcast_fusion.1
  672.0 11.6 %all-reduce.14 = (f32[4,512]{1,0:T(4,128)S(1)}, f32[1000]{0:T(1024)S(1)}) all-reduce(f32[4,512]{1,0:T(4,128)S(1)} %multiply_subtract_fusion.6, f32[1000]{0:T(1024)S(1)} %get-tuple-element.46), channel_id=1, replica_groups=mesh['rep'=4,'dp'=8] {'rep'}, use_global_device_ids=true, to_apply=%region_24.25 | all-reduce | flops 3048 | bytes 24384 | tf_op jit(solution)/shard_map/psum | solution.py:157
  685.5 34.6 %all-reduce.18.cloned.1.call-done = (f32[13,64,512]{2,1,0:T(8,128)}, f32[64,1000]{1,0:T(8,128)}) async-done(((f32[13,64,512]{2,1,0:T(8,128)}, f32[64,1000]{1,0:T(8,128)}), (f32[13,64,512]{2,1,0:T(8,128)}, f32[64,1000]{1,0:T(8,128)})) %all-reduce.18.cloned.1.call-update) | async-done | bytes 1959952 | tf_op jit(solution)/shard_map/psum | solution.py:157
  720.1 6.0 convert_multiply_fusion
  (145 shorter events, 95.5 us)
Async XLA Ops:
  7.2 119.6 %all-gather.2.cloned.1.call-start = ((), (), s32[]{:S(2)}) async-start(), calls=%async_computation.3 | async-start | bytes 7667712 | tf_op jit(solution)/shard_map/all_gather | solution.py:103
  10.6 429.1 %reduce-scatter.8.cloned.1.call-start = ((), (), s32[]{:S(2)}) async-start(), calls=%async_computation.6 | async-start | bytes 2359296 | tf_op jit(solution)/shard_map/reduce_scatter | solution.py:146
  20.0 9.6 %copy-start.13 = (f32[64,1000]{1,0:T(8,128)S(1)}, f32[64,1000]{1,0:T(8,128)}, u32[]{:S(2)}) copy-start(f32[64,1000]{1,0:T(8,128)} %param.25) | copy-start | bytes 768004
  20.0 9.6 %copy-start.20 = (f32[4,512]{1,0:T(4,128)S(1)}, f32[4,512]{1,0:T(4,128)}, u32[]{:S(2)}) copy-start(f32[4,512]{1,0:T(4,128)} %param.26) | copy-start | bytes 24580
  29.6 164.5 %copy-start.23 = (f32[1,512]{1,0:T(1,128)}, f32[1,512]{1,0:T(1,128)S(1)}, u32[]{:S(2)}) copy-start(f32[1,512]{1,0:T(1,128)S(1)} %get-tuple-element.87) | copy-start | bytes 6148
  29.6 221.0 %copy-start.25 = (f32[1,512]{1,0:T(1,128)}, f32[1,512]{1,0:T(1,128)S(1)}, u32[]{:S(2)}) copy-start(f32[1,512]{1,0:T(1,128)S(1)} %get-tuple-element.85) | copy-start | bytes 6148
  29.7 221.0 %copy-start.34 = (f32[1,512]{1,0:T(1,128)}, f32[1,512]{1,0:T(1,128)S(1)}, u32[]{:S(2)}) copy-start(f32[1,512]{1,0:T(1,128)S(1)} %get-tuple-element.86) | copy-start | bytes 6148
  250.6 4.6 copy-start.31
  276.6 25.2 %copy-start.38 = (f32[512]{0:T(512)S(1)}, f32[512]{0:T(512)}, u32[]{:S(2)}) copy-start(f32[512]{0:T(512)} %get-tuple-element.91) | copy-start | bytes 6148
  310.4 181.6 %reduce-scatter.4.cloned.1.call-start = ((), (), s32[]{:S(2)}) async-start(), calls=%async_computation.4 | async-start | bytes 4718592 | tf_op jit(solution)/shard_map/reduce_scatter | solution.py:142
  345.3 5.5 copy-start.2
  345.3 5.8 copy-start.3
  345.3 6.7 copy-start.4
  345.4 7.6 %copy-start.5 = (f32[32,7,7,512]{3,0,2,1:T(8,128)S(1)}, f32[32,7,7,512]{3,0,2,1:T(8,128)}, u32[]{:S(2)}) copy-start(f32[32,7,7,512]{3,0,2,1:T(8,128)} %get-tuple-element.63) | copy-start | bytes 9633796
  361.0 4.7 copy-start.24
  365.7 5.3 copy-start.36
  365.7 24.1 %copy-start.33 = (f32[512]{0:T(512)S(1)}, f32[512]{0:T(512)}, u32[]{:S(2)}) copy-start(f32[512]{0:T(512)} %get-tuple-element.89) | copy-start | bytes 6148
  405.2 254.3 %reduce-scatter.6.cloned.1.call-start = ((), (), s32[]{:S(2)}) async-start(), calls=%async_computation.5 | async-start | bytes 10616832 | tf_op jit(solution)/shard_map/reduce_scatter | solution.py:145
  405.2 19.4 %copy-start.11 = (bf16[1568,512]{1,0:T(8,128)(2,1)S(1)}, bf16[1568,512]{1,0:T(8,128)(2,1)}, u32[]{:S(2)}) copy-start(bf16[1568,512]{1,0:T(8,128)(2,1)} %multiply_convert_fusion) | copy-start | bytes 4816900
  438.9 220.6 %copy-start = (s32[13,64,512]{2,1,0:T(8,128)S(1)}, s32[13,64,512]{2,1,0:T(8,128)}, u32[]{:S(2)}) copy-start(s32[13,64,512]{2,1,0:T(8,128)} %param.23) | copy-start | bytes 5111812
  438.9 281.2 %all-reduce.18.cloned.1.call-start = ((), (), s32[]{:S(2)}) async-start(), calls=%async_computation.7 | async-start | bytes 3932160 | tf_op jit(solution)/shard_map/psum | solution.py:157
  659.5 5.5 copy-start.12
  659.5 5.5 copy-start.14
  659.5 5.5 copy-start.15
  665.0 6.3 copy-start.1
  665.0 7.0 copy-start.21
  665.0 6.9 copy-start.27
  665.1 6.9 copy-start.28
  665.1 18.6 %copy-start.39 = (f32[1000]{0:T(1024)S(1)}, f32[1000]{0:T(1024)}, u32[]{:S(2)}) copy-start(f32[1000]{0:T(1024)} %param.39) | copy-start | bytes 12004
  665.1 19.8 %copy-start.37 = (f32[4,512]{1,0:T(4,128)S(1)}, f32[4,512]{1,0:T(4,128)}, u32[]{:S(2)}) copy-start(f32[4,512]{1,0:T(4,128)} %param.38) | copy-start | bytes 24580
  720.1 6.0 copy-start.18
  720.1 6.0 copy-start.19
  (17 other events, 46.1 us)
Sparse Core Ops, SparseCore 0:
  10.8 115.9 all-gather.1
  310.5 65.4 reduce-scatter.7
  405.3 86.6 reduce-scatter.3
  495.9 163.5 reduce-scatter.5
  671.5 48.5 all-reduce.17
where the time goes:
time: 741 us; the launch traced here: 734 us
  waiting for transfers between devices  310 us (42%)
  local copies, waits for them, and re-layouts  152 us (21%)
  blocking collectives  126 us (17%)
  other arithmetic  68.2 us (9%)
  matrix products  63.7 us (9%)
  between operations  14.3 us (2%)
    reduce_scatter x1, waiting for transfers between devices, per_device(): lax.psum_scatter(taps_grad.reshape(9, width, width), 'dp', scatter_dimens...  168 us
    all_gather x1, waiting for transfers between devices, per_device(): lax.all_gather(effective.astype(jnp.bfloat16), 'dp', axis=1, tiled=True)  57.3 us
    reduce_scatter x1, waiting for transfers between devices, per_device(): lax.psum_scatter(first_grad.reshape(blocks, width, width), 'dp', scatter_...  50 us
    all_gather x1, blocking collectives, per_device(): lax.all_gather(head_weight.astype(jnp.bfloat16), 'dp', axis=0, tiled=True)  39.8 us
    psum x2, blocking collectives, norm_backward(): lax.psum((jnp.sum(grad_pre * normed, axis=0), jnp.sum(grad_pre, axis=0),...  37.7 us
    psum x2, blocking collectives, norm_forward(): lax.psum((jnp.sum(pre, axis=0), jnp.sum(pre * pre, axis=0)), 'dp')  36.6 us
    psum x1, waiting for transfers between devices, per_device(): lax.psum((conv_g, head_g, norm_g, bias_g), 'rep')  34.6 us
    concatenate x9, local copies, waits for them, and re-layouts, unfold(): jnp.concatenate(pieces, axis=-1)  30.7 us
  transfers between devices with their start and end apart: 5, of which 4 were waited for; matrix products, arithmetic and copies ran while one was open for 18% of the time, Pallas kernels for 0%

commit v1 on v0

v1 whole, which is shorter than its diff:
```python
import functools

import jax
import jax.numpy as jnp
from jax import lax
from jax.experimental import pallas as pl
from jax.experimental.pallas import tpu as pltpu
from jax.sharding import PartitionSpec as P

C_IN = 2048
C_MID = 512
CLASSES = 1000
WIDE = 1024
SIDE = 7
STEP = 10
PIX = 49
DROP_CUT = 78643
GROW_CUT = 242484
BF = jnp.bfloat16
F32 = jnp.float32
I32 = jnp.int32
I16 = jnp.int16
EXTRA = 16
LEVELS = 32000.0
VMEM_BYTES = 44 * 1024 * 1024


def swap(x, axis, bit):
    n = lax.axis_size(axis)
    return lax.ppermute(x, axis, [(i, i ^ bit) for i in range(n)])


def bits_of(axis):
    n = lax.axis_size(axis)
    return [1 << k for k in range(n.bit_length() - 1)]


def sum_all(x, axis):
    for bit in bits_of(axis):
        x = x + swap(x, axis, bit)
    return x


def pick(x, axis, index):
    return lax.dynamic_index_in_dim(x, index, axis, keepdims=False)


def gather_pieces(own):
    bits = bits_of("dp")
    buf, rel = own[None], [0]
    for bit in reversed(bits[2:]):
        buf = jnp.concatenate([buf, swap(buf, "dp", bit)], axis=0)
        rel = rel + [r ^ bit for r in rel]
    near = swap(buf, "dp", bits[1])
    side = swap(buf, "dp", bits[0])
    far = swap(near, "dp", bits[0])
    pieces = [buf, near, side, far]
    shifts = [0, bits[1], bits[0], bits[1] | bits[0]]
    codes = [[(0, r ^ s) for r in rel] for s in shifts]
    pieces += [swap(p, "rep", 1) for p in pieces]
    codes += [[(1, r) for _, r in c] for c in codes]
    if own.shape[1] % 16:
        return place(pieces, codes), None
    return pieces, codes


def place(pieces, codes):
    n = lax.axis_size("dp")
    flat = [c * n + r for code in codes for c, r in code]
    inverse = jnp.array([flat.index(k) for k in range(2 * n)], I32)
    me = (lax.axis_index("rep") % 2) * n + lax.axis_index("dp")
    full = jnp.take(jnp.concatenate(pieces, axis=0), inverse[jnp.arange(2 * n, dtype=I32) ^ me], axis=0)
    _, blocks, r, w = full.shape
    full = full.reshape(2, n, blocks, r, w).transpose(2, 1, 0, 3, 4)
    return [full.reshape(1, blocks, n * 2 * r, w)]


def assemble(refs, codes, me, out, blocks):
    for p, ref in enumerate(refs):
        r = ref.shape[2]
        for i in range(ref.shape[0]):
            if codes is None:
                row = 0
            else:
                c, s = codes[p][i]
                row = pl.multiple_of(((me[0] ^ s) * 2 + (me[1] ^ c)) * r, 16)
            for at, b in enumerate(blocks):
                out[at, pl.ds(row, r), :] = ref[i, b]


def code_scale(k):
    return jnp.exp2(k * (1.0 / 16.0))


def code_step(top):
    return jnp.minimum(jnp.ceil(jnp.log2(jnp.maximum(top, 1e-30)) * 16.0), 2032.0)


def code_of(x, k):
    return jnp.floor(x * (LEVELS / code_scale(k)) + 0.5).astype(I32).astype(I16)


def value_of(q, k):
    return q.astype(I32).astype(F32) * (code_scale(k.astype(I32).astype(F32)) * (1.0 / LEVELS))


def encode(x):
    top = jnp.max(jnp.abs(x), axis=1, keepdims=True)
    k = code_step(top)
    row = jnp.broadcast_to(k, (x.shape[0], EXTRA, x.shape[2])).astype(I32).astype(I16)
    return jnp.concatenate([code_of(x, k), row], axis=1)


def decode(payload):
    rows = payload.shape[1] - EXTRA
    return value_of(payload[:, :rows], payload[:, rows : rows + 1])


def split_plain(full, bit):
    b, n, r, w = full.shape
    view = full.reshape(b, n // 2, 2, r, w)
    return encode(pick(view, 2, 1 - bit).reshape(b, n // 2 * r, w)), pick(view, 2, bit)


def put_split(block, bit, send_ref, keep_ref, at):
    n, r, w = block.shape
    top = jnp.zeros((1, w), F32)
    for j in range(n // 2):
        keep_ref[at, j] = block[2 * j + bit]
        top = jnp.maximum(top, jnp.max(jnp.abs(block[2 * j + 1 - bit]), axis=0, keepdims=True))
    k = code_step(top)
    for j in range(n // 2):
        send_ref[at, j * r : (j + 1) * r, :] = code_of(block[2 * j + 1 - bit], k)
    send_ref[at, n // 2 * r :, :] = jnp.broadcast_to(k, (EXTRA, w)).astype(I32).astype(I16)


def emit(block, bit_ref, outs):
    if len(outs) == 1:
        outs[0][0] = block[...]
    else:
        put_split(block, bit_ref[0], *outs, 0)


def part_shape(n, r):
    return (n, r) if r % 16 == 0 else (1, n * r)


def split_of(outs, n, r, bit):
    if len(outs) == 2:
        return outs
    full = outs[0]
    return split_plain(full.reshape(full.shape[0], n, r, full.shape[-1]), bit)


def split_shapes(blocks, n, r, w):
    if r % 16:
        return [jax.ShapeDtypeStruct((blocks, 1, n * r, w), F32)]
    return [
        jax.ShapeDtypeStruct((blocks, n // 2 * r + EXTRA, w), I16),
        jax.ShapeDtypeStruct((blocks, n // 2, r, w), F32),
    ]


def add_split_kernel(bit_ref, keep_in, got, send_ref, keep_ref, total):
    n, r = keep_in.shape[1:3]
    k = got[0, n * r : n * r + 16, :][0:1]
    for j in range(n):
        total[j] = keep_in[0, j] + value_of(got[0, j * r : (j + 1) * r, :], k)
    put_split(total, bit_ref[0], send_ref, keep_ref, 0)


def add_split(keep, got, bit):
    b, n, r, w = keep.shape
    if r % 16:
        return split_plain(keep + decode(got).reshape(keep.shape), bit)
    one = lambda shape: pl.BlockSpec((1,) + shape, lambda i: (i,) + (0,) * len(shape))
    return pl.pallas_call(
        add_split_kernel,
        grid=(b,),
        in_specs=[
            pl.BlockSpec(memory_space=pltpu.SMEM), one((n, r, w)), one((n * r + EXTRA, w)),
        ],
        out_specs=[one((n // 2 * r + EXTRA, w)), one((n // 2, r, w))],
        out_shape=split_shapes(b, n, r, w),
        scratch_shapes=[pltpu.VMEM((n, r, w), F32)],
        name="add_split",
    )(bit.reshape(1), keep, got)


def scatter(send, keep, bits):
    me = lax.axis_index("dp")
    for at, bit in enumerate(bits):
        got = swap(send, "dp", bit)
        if at == len(bits) - 1:
            return keep[:, 0] + decode(got)
        send, keep = add_split(keep, got, (me // bits[at + 1]) % 2)


def norm_of(y, sums, gain, shift, total):
    mean = sums[0:1] * (1.0 / total)
    var = sums[1:2] * (1.0 / total) - mean * mean
    rstd = lax.rsqrt(var + 1e-05)
    n = (y - mean) * rstd
    return n, gain * n + shift, rstd


def sigmoid(z):
    return 1.0 / (1.0 + jnp.exp(-z))


def silu_grad(z):
    sig = sigmoid(z)
    return sig * (1.0 + z * (1.0 - sig))


def flat(x):
    return x.reshape(-1, x.shape[-1])


SMEM = pl.BlockSpec(memory_space=pltpu.SMEM)
PARAMS = pltpu.CompilerParams(vmem_limit_bytes=VMEM_BYTES)


def whole(shape):
    return pl.BlockSpec(tuple(shape), lambda *_: (0,) * len(shape))


def cost(flops, byte_count):
    return pl.CostEstimate(flops=int(flops), bytes_accessed=int(byte_count), transcendentals=0)


def first_kernel(codes, count, me, x, *refs):
    pieces, (y, sums, weights) = refs[:count], refs[count:]
    step = pl.program_id(0)

    @pl.when(step == 0)
    def _():
        assemble(pieces, codes, me, weights, range(weights.shape[0]))
        sums[...] = jnp.zeros_like(sums)

    out = jnp.dot(x[0], weights[...].reshape(-1, C_MID), preferred_element_type=F32)
    y[0] = out
    sums[0:1] += jnp.sum(out, axis=0, keepdims=True)
    sums[1:2] += jnp.sum(out * out, axis=0, keepdims=True)


def first_forward(me, x, pieces, codes):
    rows = x.shape[1]
    blocks = C_IN // C_MID
    return pl.pallas_call(
        functools.partial(first_kernel, codes, len(pieces)),
        grid=(SIDE,),
        in_specs=[SMEM, pl.BlockSpec((1, rows, C_IN), lambda i: (i, 0, 0))]
        + [whole(p.shape) for p in pieces],
        out_specs=[pl.BlockSpec((1, rows, C_MID), lambda i: (i, 0, 0)), whole((2, C_MID))],
        out_shape=[
            jax.ShapeDtypeStruct((SIDE, rows, C_MID), F32),
            jax.ShapeDtypeStruct((2, C_MID), F32),
        ],
        scratch_shapes=[pltpu.VMEM((blocks, C_MID, C_MID), BF)],
        compiler_params=PARAMS,
        cost_estimate=cost(2 * SIDE * rows * C_IN * C_MID, 12e6),
        name="first_forward",
    )(me, x, *pieces)


def second_kernel(codes, count, total, me, y1, sums1, params, *refs):
    pieces, (h1, y2, sums2, pad, taps) = refs[:count], refs[count:]
    step = pl.program_id(0)
    batch = pad.shape[2]

    @pl.when(step == 0)
    def _():
        pad[...] = jnp.zeros_like(pad)
        assemble(pieces, codes, me, taps, range(9))
        sums2[...] = jnp.zeros_like(sums2)

    @pl.when(step < SIDE)
    def _():
        _, z, _ = norm_of(y1[0], sums1[...], params[0:1], params[1:2], total)
        h = (z * sigmoid(z)).astype(BF)
        h1[0] = h
        pad[step + 1, 1 : SIDE + 1] = h.reshape(SIDE, batch, C_MID)

    @pl.when(step > 0)
    def _():
        out = None
        for a in range(3):
            patch = jnp.concatenate(
                [flat(pad[step - 1 + a, b : b + SIDE]) for b in range(3)], axis=1
            )
            part = jnp.dot(
                patch, taps[3 * a : 3 * a + 3].reshape(3 * C_MID, C_MID), preferred_element_type=F32
            )
            out = part if out is None else out + part
        y2[0] = out
        sums2[0:1] += jnp.sum(out, axis=0, keepdims=True)
        sums2[1:2] += jnp.sum(out * out, axis=0, keepdims=True)


def second_forward(me, y1, sums1, params, pieces, codes, total):
    rows = y1.shape[1]
    batch = rows // SIDE
    row = lambda f: pl.BlockSpec((1, rows, C_MID), lambda i: (f(i), 0, 0))
    here = row(lambda i: jnp.minimum(i, SIDE - 1))
    return pl.pallas_call(
        functools.partial(second_kernel, codes, len(pieces), total),
        grid=(SIDE + 1,),
        in_specs=[SMEM, here, whole(sums1.shape), whole(params.shape)] + [whole(p.shape) for p in pieces],
        out_specs=[here, row(lambda i: jnp.maximum(i - 1, 0)), whole((2, C_MID))],
        out_shape=[
            jax.ShapeDtypeStruct((SIDE, rows, C_MID), BF),
            jax.ShapeDtypeStruct((SIDE, rows, C_MID), F32),
            jax.ShapeDtypeStruct((2, C_MID), F32),
        ],
        scratch_shapes=[
            pltpu.VMEM((SIDE + 2, SIDE + 2, batch, C_MID), BF),
            pltpu.VMEM((9, C_MID, C_MID), BF),
        ],
        compiler_params=PARAMS,
        cost_estimate=cost(2 * SIDE * rows * 9 * C_MID * C_MID, 14e6),
        name="second_forward",
    )(me, y1, sums1, params, *pieces)


def head_kernel(codes, count, total, group_images, me, y2, sums2, params, bias, labels, *refs):
    pieces, (grad, packed, dpool_out, head, sum_h, sum_a, sum_b) = refs[:count], refs[count:]
    step = pl.program_id(0)
    batch = sum_h.shape[0]

    @pl.when(step == 0)
    def _():
        assemble(pieces, codes, me, head, (9, 10))
        for ref in (sum_h, sum_a, sum_b):
            ref[...] = jnp.zeros_like(ref)

    n, z, _ = norm_of(y2[0], sums2[...], params[2:3], params[3:4], total)
    sig = sigmoid(z)
    slope = sig * (1.0 + z * (1.0 - sig))
    fold = lambda v: jnp.sum(v.reshape(SIDE, batch, C_MID), axis=0)
    sum_h[...] += fold(z * sig)
    sum_a[...] += fold(slope)
    sum_b[...] += fold(slope * n)

    @pl.when(step == SIDE - 1)
    def _():
        pooled = (sum_h[...] * (1.0 / PIX)).astype(BF)
        logits = jnp.concatenate(
            [jnp.dot(pooled, head[k], preferred_element_type=F32) for k in range(2)], axis=1
        )
        logits = logits + bias[...]
        column = lax.broadcasted_iota(I32, (batch, WIDE), 1)
        logits = jnp.where(column < CLASSES, logits, -1e30)
        onehot = (labels[...] == column).astype(F32)
        top = jnp.max(logits, axis=1, keepdims=True)
        expo = jnp.exp(logits - top)
        expsum = jnp.sum(expo, axis=1, keepdims=True)
        lse = top + jnp.log(expsum)
        loss = jnp.sum(lse - jnp.sum(logits * onehot, axis=1, keepdims=True), axis=0, keepdims=True)
        dlogits = ((jnp.exp(logits - lse) - onehot) * (1.0 / group_images)).astype(BF)
        bias_sum = jnp.sum(dlogits.astype(F32), axis=0, keepdims=True)
        last = lax.broadcasted_iota(I32, (1, WIDE), 1) == WIDE - 1
        bias_sum = jnp.where(last, loss, bias_sum)
        dpool = jnp.zeros((batch, C_MID), F32)
        for k in range(2):
            part = dlogits[:, k * C_MID : (k + 1) * C_MID]
            grad[k] = lax.dot_general(
                pooled, part, (((0,), (0,)), ((), ())), preferred_element_type=F32
            )
            dpool = dpool + lax.dot_general(
                part, head[k], (((1,), (1,)), ((), ())), preferred_element_type=F32
            )
        dpool = dpool * (1.0 / PIX)
        dpool_out[...] = dpool
        packed[0:1] = jnp.sum(dpool * sum_b[...], axis=0, keepdims=True)
        packed[1:2] = jnp.sum(dpool * sum_a[...], axis=0, keepdims=True)
        packed[2:3] = bias_sum[:, :C_MID]
        packed[3:4] = bias_sum[:, C_MID:]


def head_step(me, y2, sums2, params, bias, labels, pieces, codes, total, group_images):
    rows = y2.shape[1]
    batch = rows // SIDE
    return pl.pallas_call(
        functools.partial(head_kernel, codes, len(pieces), total, group_images),
        grid=(SIDE,),
        in_specs=[
            SMEM, pl.BlockSpec((1, rows, C_MID), lambda i: (i, 0, 0)), whole(sums2.shape),
            whole(params.shape), whole(bias.shape), whole(labels.shape),
        ] + [whole(p.shape) for p in pieces],
        out_specs=[whole((2, C_MID, C_MID)), whole((4, C_MID)), whole((batch, C_MID))],
        out_shape=[
            jax.ShapeDtypeStruct((2, C_MID, C_MID), F32),
            jax.ShapeDtypeStruct((4, C_MID), F32),
            jax.ShapeDtypeStruct((batch, C_MID), F32),
        ],
        scratch_shapes=[pltpu.VMEM((2, C_MID, C_MID), BF)] + [pltpu.VMEM((batch, C_MID), F32)] * 3,
        compiler_params=PARAMS,
        cost_estimate=cost(40e6, 10e6),
        name="head_step",
    )(me, y2, sums2, params, bias, labels, *pieces)


def taps_kernel(total, first_tap, count, bit_ref, y2, sums2, back, params, dpool, h1, dy_out, turned, *refs):
    outs, (pad, block) = refs[:-2], refs[-2:]
    step = pl.program_id(0)
    batch = pad.shape[2]

    @pl.when(step == 0)
    def _():
        pad[...] = jnp.zeros_like(pad)
        turned[...] = h1[...].T

    @pl.when(step < SIDE)
    def _():
        n, z, rstd = norm_of(y2[0], sums2[...], params[2:3], params[3:4], total)
        dz = silu_grad(z).reshape(SIDE, batch, C_MID) * dpool[...][None]
        dz = flat(dz)
        dy = params[2:3] * rstd * (dz - back[1:2] * (1.0 / total) - n * (back[0:1] * (1.0 / total)))
        pad[step + 1, 1 : SIDE + 1] = dy.astype(BF).reshape(SIDE, batch, C_MID)

    @pl.when(step == SIDE - 1)
    def _():
        dy_out[...] = pad[...]

    @pl.when(step >= SIDE)
    def _():
        tap = step - SIDE + first_tap
        one_tap(tap, pad, turned, bit_ref, block, outs)


def one_tap(tap, pad, turned, bit_ref, block, outs):
    a, b = tap // 3, tap % 3
    moved = flat(pad[pl.ds(2 - a, SIDE), pl.ds(2 - b, SIDE)].reshape(-1, C_MID))
    block[...] = jnp.dot(turned[...], moved, preferred_element_type=F32).reshape(block.shape)
    emit(block, bit_ref, outs)


def taps_more_kernel(first_tap, bit_ref, pad, turned, *refs):
    one_tap(pl.program_id(0) + first_tap, pad, turned, bit_ref, refs[-1], refs[:-1])


def split_specs(n, r, f):
    if r % 16:
        return [pl.BlockSpec((1, 1, n * r, C_MID), lambda i: (f(i), 0, 0, 0))]
    return [
        pl.BlockSpec((1, n // 2 * r + EXTRA, C_MID), lambda i: (f(i), 0, 0)),
        pl.BlockSpec((1, n // 2, r, C_MID), lambda i: (f(i), 0, 0, 0)),
    ]


def taps_grad_first(bit, y2, sums2, back, params, dpool, h1, total, n, r, first_tap, count):
    rows = y2.shape[1]
    batch = rows // SIDE
    padded = (SIDE + 2, SIDE + 2, batch, C_MID)
    return pl.pallas_call(
        functools.partial(taps_kernel, total, first_tap, count),
        grid=(SIDE + count,),
        in_specs=[
            SMEM, pl.BlockSpec((1, rows, C_MID), lambda i: (jnp.minimum(i, SIDE - 1), 0, 0)),
            whole(sums2.shape), whole(back.shape), whole(params.shape), whole(dpool.shape),
            whole(h1.shape),
        ],
        out_specs=[whole(padded), whole((C_MID, h1.shape[0]))]
        + split_specs(n, r, lambda i: jnp.maximum(i - SIDE, 0)),
        out_shape=[
            jax.ShapeDtypeStruct(padded, BF), jax.ShapeDtypeStruct((C_MID, h1.shape[0]), BF),
        ] + split_shapes(count, n, r, C_MID),
        scratch_shapes=[pltpu.VMEM(padded, BF), pltpu.VMEM(part_shape(n, r) + (C_MID,), F32)],
        compiler_params=PARAMS,
        cost_estimate=cost(2 * SIDE * rows * count * C_MID * C_MID, 14e6),
        name="taps_grad_first",
    )(bit.reshape(1), y2, sums2, back, params, dpool, h1)


def taps_grad_more(bit, pad, turned, n, r, first_tap, count):
    return pl.pallas_call(
        functools.partial(taps_more_kernel, first_tap),
        grid=(count,),
        in_specs=[SMEM, whole(pad.shape), whole(turned.shape)],
        out_specs=split_specs(n, r, lambda i: i),
        out_shape=split_shapes(count, n, r, C_MID),
        scratch_shapes=[pltpu.VMEM(part_shape(n, r) + (C_MID,), F32)],
        compiler_params=PARAMS,
        cost_estimate=cost(2 * turned.shape[1] * count * C_MID * C_MID, 10e6),
        name="taps_grad_more",
    )(bit.reshape(1), pad, turned)


def input_grad_kernel(codes, count, total, me, pad, y1, sums1, params, *refs):
    pieces, (dz1, sums, taps) = refs[:count], refs[count:]
    step = pl.program_id(0)

    @pl.when(step == 0)
    def _():
        assemble(pieces, codes, me, taps, range(9))
        sums[...] = jnp.zeros_like(sums)

    dh = None
    for a in range(3):
        for b in range(3):
            part = lax.dot_general(
                flat(pad[step + 2 - a, 2 - b : 2 - b + SIDE]), taps[3 * a + b],
                (((1,), (1,)), ((), ())), preferred_element_type=F32,
            )
            dh = part if dh is None else dh + part
    n, z, _ = norm_of(y1[0], sums1[...], params[0:1], params[1:2], total)
    dz = dh * silu_grad(z)
    dz1[0] = dz
    sums[0:1] += jnp.sum(dz * n, axis=0, keepdims=True)
    sums[1:2] += jnp.sum(dz, axis=0, keepdims=True)


def input_grad(me, pad, y1, sums1, params, pieces, codes, total):
    rows = y1.shape[1]
    row = pl.BlockSpec((1, rows, C_MID), lambda i: (i, 0, 0))
    return pl.pallas_call(
        functools.partial(input_grad_kernel, codes, len(pieces), total),
        grid=(SIDE,),
        in_specs=[SMEM, whole(pad.shape), row, whole(sums1.shape), whole(params.shape)]
        + [whole(p.shape) for p in pieces],
        out_specs=[row, whole((2, C_MID))],
        out_shape=[
            jax.ShapeDtypeStruct(y1.shape, F32), jax.ShapeDtypeStruct((2, C_MID), F32),
        ],
        scratch_shapes=[pltpu.VMEM((9, C_MID, C_MID), BF)],
        compiler_params=PARAMS,
        cost_estimate=cost(2 * SIDE * rows * 9 * C_MID * C_MID, 16e6),
        name="input_grad",
    )(me, pad, y1, sums1, params, *pieces)


def first_grad_kernel(total, bit_ref, dz1, y1, sums1, back, params, x, dy_out, *refs):
    step = pl.program_id(0)

    @pl.when(step < SIDE)
    def _():
        n, _, rstd = norm_of(y1[0], sums1[...], params[0:1], params[1:2], total)
        dy = params[0:1] * rstd * (
            dz1[0] - back[1:2] * (1.0 / total) - n * (back[0:1] * (1.0 / total))
        )
        dy_out[step] = dy.astype(BF)

    @pl.when(step >= SIDE)
    def _():
        one_first(x, dy_out, bit_ref, refs[-1], refs[:-1])


def one_first(x, dy, bit_ref, block, outs):
    block[...] = lax.dot_general(
        flat(x[...]), flat(dy[...]), (((0,), (0,)), ((), ())), preferred_element_type=F32
    ).reshape(block.shape)
    emit(block, bit_ref, outs)


def first_more_kernel(bit_ref, x, dy, *refs):
    one_first(x, dy, bit_ref, refs[-1], refs[:-1])


def first_grad_first(bit, dz1, y1, sums1, back, params, x, total, n, r, count):
    rows = y1.shape[1]
    row = pl.BlockSpec((1, rows, C_MID), lambda i: (jnp.minimum(i, SIDE - 1), 0, 0))
    here = lambda i: jnp.maximum(i - SIDE, 0)
    return pl.pallas_call(
        functools.partial(first_grad_kernel, total),
        grid=(SIDE + count,),
        in_specs=[
            SMEM, row, row, whole(sums1.shape), whole(back.shape), whole(params.shape),
            pl.BlockSpec((SIDE, rows, C_MID), lambda i: (0, 0, here(i))),
        ],
        out_specs=[whole((SIDE, rows, C_MID))] + split_specs(n, r, here),
        out_shape=[jax.ShapeDtypeStruct((SIDE, rows, C_MID), BF)] + split_shapes(count, n, r, C_MID),
        scratch_shapes=[pltpu.VMEM(part_shape(n, r) + (C_MID,), F32)],
        compiler_params=PARAMS,
        cost_estimate=cost(2 * SIDE * rows * count * C_MID * C_MID, 14e6),
        name="first_grad_first",
    )(bit.reshape(1), dz1, y1, sums1, back, params, x)


def first_grad_more(bit, x, dy, n, r, first_block, count):
    rows = dy.shape[1]
    return pl.pallas_call(
        first_more_kernel,
        grid=(count,),
        in_specs=[
            SMEM, pl.BlockSpec((SIDE, rows, C_MID), lambda i: (0, 0, i + first_block)), whole(dy.shape),
        ],
        out_specs=split_specs(n, r, lambda i: i),
        out_shape=split_shapes(count, n, r, C_MID),
        scratch_shapes=[pltpu.VMEM(part_shape(n, r) + (C_MID,), F32)],
        compiler_params=PARAMS,
        cost_estimate=cost(2 * SIDE * rows * count * C_MID * C_MID, 8e6),
        name="first_grad_more",
    )(bit.reshape(1), x, dy)


def adamw(weight, grad, first, second, rate):
    first = 0.9 * first + 0.1 * grad
    second = 0.999 * second + 0.001 * grad * grad
    normal_step = first / (1.0 - 0.9**STEP) / (jnp.sqrt(second / (1.0 - 0.999**STEP)) + 1e-08)
    return (-rate * (normal_step + 0.01 * weight), first, second)


def outer_step(start, step_sum, momentum, groups):
    delta = -(step_sum / groups)
    momentum = 0.9 * momentum + delta
    return (start - 0.7 * (delta + 0.9 * momentum), momentum)


def rep_sum(x):
    for bit in bits_of("rep"):
        low = x.astype(BF)
        x = low.astype(F32) + swap(low, "rep", bit).astype(F32)
    return x


def per_device(
    images, labels, conv_weight, conv_mask, conv_rank, head_weight, norm_params, head_bias,
    conv_first, conv_second, head_first, head_second, norm_first, norm_second, bias_first,
    bias_second, conv_outer, head_outer, norm_outer, bias_outer,
):
    devices = lax.axis_size("dp")
    groups = lax.axis_size("rep")
    width = C_MID
    blocks = C_IN // C_MID
    core = lax.axis_index("rep") % 2
    dp = lax.axis_index("dp")
    me = jnp.stack([dp, core]).astype(I32)
    bits = bits_of("dp")
    bit = dp % 2
    shard = conv_weight.shape[1]
    batch = images.shape[0]
    rows = batch * PIX
    total = float(rows * devices)
    group_images = batch * devices
    half = shard // 2

    def mine(x):
        return pick(x.reshape(-1, 2, half, width), 1, core)

    def active(sl):
        return jnp.where(mine(conv_mask[sl]) == 1, mine(conv_weight[sl]), 0.0).astype(BF)

    head_wide = jnp.pad(head_weight.astype(BF), ((0, 0), (0, WIDE - CLASSES)))
    head_low = mine(head_wide.reshape(shard, 2, width).transpose(1, 0, 2))
    first_pieces, first_codes = gather_pieces(active(slice(0, blocks)))
    rest = jnp.concatenate([active(slice(blocks, None)), head_low], axis=0)
    taps_pieces, taps_codes = gather_pieces(rest)
    x = images.transpose(1, 2, 0, 3).reshape(SIDE, SIDE * batch, C_IN)
    y_one, sums_one = first_forward(me, x, first_pieces, first_codes)
    sums_one = sum_all(sums_one, "dp")
    h_one, y_two, sums_two = second_forward(
        me, y_one, sums_one, norm_params, taps_pieces, taps_codes, total
    )
    sums_two = sum_all(sums_two, "dp")
    bias_wide = jnp.pad(head_bias, (0, WIDE - CLASSES)).reshape(1, WIDE)
    head_local, packed, dpool = head_step(
        me, y_two, sums_two, norm_params, bias_wide, labels[:, None], taps_pieces, taps_codes, total,
        group_images,
    )
    packed = sum_all(packed, "dp")
    bias_grad = packed[2:].reshape(-1)[:CLASSES]
    loss_sum = packed[3, C_MID - 1 :]
    head_send, head_keep = split_plain(head_local.reshape(2, devices, shard, width), bit)
    cut = 4
    n, r = devices, shard
    grads = {}
    pad, turned, *outs = taps_grad_first(
        bit, y_two, sums_two, packed, norm_params, dpool, flat(h_one), total, n, r, 0, cut
    )
    grads["taps_a"] = (*split_of(outs, n, r, bit), blocks)
    outs = taps_grad_more(bit, pad, turned, n, r, cut, 9 - cut)
    grads["taps_b"] = (*split_of(outs, n, r, bit), blocks + cut)
    dz_one, back_one = input_grad(
        me, pad, y_one, sums_one, norm_params, taps_pieces, taps_codes, total
    )
    back_one = sum_all(back_one, "dp")
    dy_one, *outs = first_grad_first(
        bit, dz_one, y_one, sums_one, back_one, norm_params, x, total, n, r, 2
    )
    grads["first_a"] = (*split_of(outs, n, r, bit), 0)
    outs = first_grad_more(bit, x, dy_one, n, r, 2, 2)
    grads["first_b"] = (*split_of(outs, n, r, bit), 2)

    mask_old = conv_mask.astype(F32)
    dropped = (conv_mask == 1) & (conv_rank < DROP_CUT)
    grown = (conv_mask == 0) & (conv_rank >= GROW_CUT)
    mask_int = jnp.where(dropped, 0, jnp.where(grown, 1, conv_mask))
    mask_new = mask_int.astype(F32)
    kept = mask_old * mask_new
    effective = conv_weight * mask_old
    start = conv_weight * kept
    head_grad = scatter(head_send, head_keep, bits)
    head_grad = head_grad.transpose(1, 0, 2).reshape(shard, WIDE)[:, :CLASSES]
    done = {}
    for send, keep, at in grads.values():
        count = keep.shape[0]
        sl = slice(at, at + count)
        owned = scatter(send, keep, bits)
        dense = owned + 5e-05 * effective[sl]
        step, m, v = adamw(
            start[sl], mask_new[sl] * dense, conv_first[0, sl] * kept[sl],
            conv_second[0, sl] * kept[sl], 0.03
        )
        new, mom = outer_step(start[sl], rep_sum(step * mask_new[sl]), conv_outer[sl], groups)
        done[at] = (new * mask_new[sl], m * mask_new[sl], v * mask_new[sl], mom * mask_new[sl])
    conv_new, conv_m, conv_v, conv_mom = (
        jnp.concatenate([done[at][k] for at in sorted(done)], axis=0) for k in range(4)
    )
    norm_grad = jnp.concatenate([back_one, packed[:2]], axis=0)
    head_s, head_m, head_v = adamw(head_weight, head_grad, head_first[0], head_second[0], 0.03)
    head_new, head_mom = outer_step(head_weight, rep_sum(head_s), head_outer, groups)
    norm_s, norm_m, norm_v = adamw(norm_params, norm_grad, norm_first[0], norm_second[0], 0.3)
    bias_s, bias_m, bias_v = adamw(head_bias, bias_grad, bias_first[0], bias_second[0], 0.3)
    small = jnp.concatenate([norm_s.reshape(-1), bias_s, jnp.zeros((24,), F32)]).reshape(-1, 128)
    small = sum_all(small, "rep").reshape(-1)
    norm_new, norm_mom = outer_step(norm_params, small[: 4 * width].reshape(4, width), norm_outer, groups)
    bias_new, bias_mom = outer_step(head_bias, small[4 * width : 4 * width + CLASSES], bias_outer, groups)
    return (
        conv_new, mask_int, conv_m[None], conv_v[None], conv_mom,
        head_new, head_m[None], head_v[None], head_mom,
        norm_new, norm_m[None], norm_v[None], norm_mom,
        bias_new, bias_m[None], bias_v[None], bias_mom, loss_sum,
    )
def solution(mesh):
    conv = P(None, "dp", None)
    conv_rep = P("rep", None, "dp", None)
    head = P("dp", None)
    head_rep = P("rep", "dp", None)
    in_specs = (
        P(("rep", "dp"), None, None, None), P(("rep", "dp")), conv, conv, conv, head, P(), P(),
        conv_rep, conv_rep, head_rep, head_rep, P("rep", None, None), P("rep", None, None),
        P("rep", None), P("rep", None), conv, head, P(), P(),
    )
    out_specs = (
        conv, conv, conv_rep, conv_rep, conv, head, head_rep, head_rep, head,
        P(), P("rep", None, None), P("rep", None, None), P(),
        P(), P("rep", None), P("rep", None), P(), P("rep"),
    )
    return jax.shard_map(
        per_device, mesh=mesh, in_specs=in_specs, out_specs=out_specs, check_vma=False
    )
```

time: 741 us -> 363 us (0.49)
  waiting for transfers between devices: 310 us -> 135 us
  blocking collectives: 126 us -> 0 us
  local copies, waits for them, and re-layouts: 152 us -> 26.9 us
  Pallas kernels: 0 us -> 99.3 us
  matrix products: 63.7 us -> 0 us
  starting transfers between devices: 0.61 us -> 61 us
  other arithmetic: 68.2 us -> 37.1 us
  between operations: 14.3 us -> 1.53 us
    reduce_scatter x3 -> x0, waiting for transfers between devices: 218 us -> none  [the longest x1 168 us: per_device(): lax.psum_scatter(taps_grad.reshape(9, width, width), 'dp', scatter_dimens...]
    ppermute x0 -> x55, waiting for transfers between devices: none -> 135 us  [swap(): return lax.ppermute(x, axis, [(i, i ^ bit) for i in range(n)])]
    pallas_call x0 -> x18, Pallas kernels: none -> 99.3 us  [the longest x10 29.3 us: add_split(): pl.pallas_call(add_split_kernel, grid=(b,), in_specs=[pl.BlockSpec(memory...]
    psum x5 -> x0, blocking collectives: 85.9 us -> none  [the longest x2 37.7 us: norm_backward(): lax.psum((jnp.sum(grad_pre * normed, axis=0), jnp.sum(grad_pre, axis=0),...]
    dot_general x8 -> x0, matrix products: 63.7 us -> none  [the longest x1 16.1 us: per_device(): dpatches = jnp.dot(dy_two, taps.T, preferred_element_type=jnp.float32)]
    ppermute x0 -> x55, starting transfers between devices: none -> 61 us  [swap(): return lax.ppermute(x, axis, [(i, i ^ bit) for i in range(n)])]
    all_gather x1 -> x0, waiting for transfers between devices: 57.3 us -> none  [per_device(): lax.all_gather(effective.astype(jnp.bfloat16), 'dp', axis=1, tiled=True)]
    all_gather x1 -> x0, blocking collectives: 39.8 us -> none  [per_device(): lax.all_gather(head_weight.astype(jnp.bfloat16), 'dp', axis=0, tiled=True)]
  transfers between devices with their start and end apart: 5 -> 55, of which waited for: 4 -> 27; matrix products, arithmetic and copies ran while one was open for 18% -> 10% of each run, Pallas kernels for 0% -> 22%
where the time goes in v1:
time: 363 us; the launch traced here: 361 us
  waiting for transfers between devices  135 us (37%)
  Pallas kernels  99.3 us (27%)
  starting transfers between devices  61 us (17%)
  other arithmetic  37.1 us (10%)
  local copies, waits for them, and re-layouts  26.9 us (7%)
    ppermute x55, waiting for transfers between devices, swap(): return lax.ppermute(x, axis, [(i, i ^ bit) for i in range(n)])  135 us
    ppermute x55, starting transfers between devices, swap(): return lax.ppermute(x, axis, [(i, i ^ bit) for i in range(n)])  61 us
    pallas_call x10, Pallas kernels, add_split(): pl.pallas_call(add_split_kernel, grid=(b,), in_specs=[pl.BlockSpec(memory...  29.3 us
    unnamed x133, local copies, waits for them, and re-layouts  22.3 us
    pallas_call x1, Pallas kernels, input_grad(): pl.pallas_call(functools.partial(input_grad_kernel, codes, len(pieces), t...  14 us
    pallas_call x1, Pallas kernels, second_forward(): pl.pallas_call(functools.partial(second_kernel, codes, len(pieces), total...  13.2 us
    pallas_call x1, Pallas kernels, taps_grad_first(): pl.pallas_call(functools.partial(taps_kernel, total, first_tap, count), g...  12.6 us
    pallas_call x1, Pallas kernels, first_forward(): pl.pallas_call(functools.partial(first_kernel, codes, len(pieces)), grid=...  8.17 us
  transfers between devices with their start and end apart: 55, of which 27 were waited for; matrix products, arithmetic and copies ran while one was open for 10% of the time, Pallas kernels for 22%

profile of v1, /device:TPU:0, one launch (start us, length us, event | category | flops | bytes accessed | tf_op | source)
XLA Modules:
  0.0 360.9 jit_solution(8212441212306564167)
XLA Ops:
  2.5 4.1 %collective-permute-start.11 = (bf16[1,11,32,512]{3,2,1,0:T(8,128)(2,1)S(1)}, bf16[1,11,32,512]{3,2,1,0:T(8,128)(2,1)S(1)}, u32[]{:S(2)}, u32[]{:S(2)}) collective-permute-start(bf16[1,11,32,512]{3,2,1,0:T(8,128)(2,1)S(1)} %maximum_bitcast_fusion.2), channel_id=1, source_target_pairs={{0,4},{1,5},{2,6},{3,7},{4,0},{5,1},{6,2},{7,3},{8,12},{9,13},{10,... | collective-permute-start | bytes 1081352 | tf_op jit(solution)/shard_map/ppermute | solution.py:30
  6.6 16.1 %collective-permute-done.11 = bf16[1,11,32,512]{3,2,1,0:T(8,128)(2,1)S(1)} collective-permute-done((bf16[1,11,32,512]{3,2,1,0:T(8,128)(2,1)S(1)}, bf16[1,11,32,512]{3,2,1,0:T(8,128)(2,1)S(1)}, u32[]{:S(2)}, u32[]{:S(2)}) %collective-permute-start.11) | collective-permute-done | bytes 360480 | tf_op jit(solution)/shard_map/ppermute | solution.py:30
  24.8 3.4 collective-permute-start
  29.7 13.3 %collective-permute-done.12.refs_1_ = bf16[2,11,32,512]{3,2,1,0:T(8,128)(2,1)S(1)} collective-permute-done((bf16[2,11,32,512]{3,2,1,0:T(8,128)(2,1)S(1)}, bf16[2,11,32,512]{3,2,1,0:T(8,128)(2,1)S(1)}, u32[]{:S(2)}, u32[]{:S(2)}) %collective-permute-start.12) | collective-permute-done | bytes 720928 | tf_op jit(solution)/shard_map/ppermute | solution.py:30
  47.8 4.4 %collective-permute-done.1.refs_1_ = bf16[2,4,32,512]{3,2,1,0:T(8,128)(2,1)S(1)} collective-permute-done((bf16[2,4,32,512]{3,2,1,0:T(8,128)(2,1)S(1)}, bf16[2,4,32,512]{3,2,1,0:T(8,128)(2,1)S(1)}, u32[]{:S(2)}, u32[]{:S(2)}) %collective-permute-start.1) | collective-permute-done | bytes 262176 | tf_op jit(solution)/shard_map/ppermute | solution.py:30
  53.7 14.7 %collective-permute-done.2.refs_2_ = bf16[2,4,32,512]{3,2,1,0:T(8,128)(2,1)} collective-permute-done((bf16[2,4,32,512]{3,2,1,0:T(8,128)(2,1)S(1)}, bf16[2,4,32,512]{3,2,1,0:T(8,128)(2,1)}, u32[]{:S(2)}, u32[]{:S(2)}) %collective-permute-start.2) | collective-permute-done | bytes 262176 | tf_op jit(solution)/shard_map/ppermute | solution.py:30
  69.7 2.8 collective-permute-done.3.refs_3_
  75.6 8.2 %first_forward.1 = (f32[7,224,512]{2,1,0:T(8,128)S(1)}, f32[2,512]{1,0:T(2,128)S(1)}) custom-call(s32[2]{0:T(128)S(1)} %pad_add_fusion.1.me, bf16[7,224,2048]{2,1,0:T(8,128)(2,1)} %bitcast.243, bf16[2,4,32,512]{3,2,1,0:T(8,128)(2,1)S(1)} %pad_maximum_fusion.3.refs_0_, bf16[2,4,32,512]{3,2,1,0:T(8,128)(2,1)S(1)} %collective-permute-done.1.refs_1_, ...), custom_call_target="tpu_custom_call" | custom-call | flops 3288334336 | bytes 12000000 | tf_op jit(solution)/shard_map/first_forward/pallas_call | solution.py:250
  87.8 3.3 collective-permute-done.9
  95.7 13.2 %second_forward.1 = (bf16[7,224,512]{2,1,0:T(8,128)(2,1)S(1)}, f32[7,224,512]{2,1,0:T(8,128)}, f32[2,512]{1,0:T(2,128)S(1)}) custom-call(s32[2]{0:T(128)S(1)} %pad_add_fusion.1.me, f32[7,224,512]{2,1,0:T(8,128)} %copy-done.1, f32[2,512]{1,0:T(2,128)S(1)} %add.306.sums1, f32[4,512]{1,0:T(4,128)S(1)} %copy-done.20, ...), custom_call_target="tpu_custom_call" | custom-call | flops 7398752256 | bytes 14000000 | tf_op jit(solution)/shard_map/second_forward/pallas_call | solution.py:306
  110.6 3.1 fusion.73
  126.3 6.6 %head_step.1 = (f32[2,512,512]{2,1,0:T(8,128)S(1)}, f32[4,512]{1,0:T(4,128)S(1)}, f32[32,512]{1,0:T(8,128)S(1)}) custom-call(s32[2]{0:T(128)S(1)} %pad_add_fusion.1.me, f32[7,224,512]{2,1,0:T(8,128)} %get-tuple-element.61.y2, f32[2,512]{1,0:T(2,128)S(1)} %add.309.sums2, f32[4,512]{1,0:T(4,128)S(1)} %copy-done.20, f32[1,1024]{1,0:T(1,128)S(1)} %bitcast.249, ...), custom_call_target="tpu_custom_call" | custom-call | flops 40000000 | bytes 10000000 | tf_op jit(solution)/shard_map/head_step/pallas_call | solution.py:384
  133.9 2.9 collective-permute-done.22
  145.6 12.6 %taps_grad_first.1 = (bf16[9,9,32,512]{3,2,1,0:T(8,128)(2,1)S(1)}, bf16[512,1568]{1,0:T(8,128)(2,1)S(1)}, s16[4,272,512]{2,1,0:T(8,128)(2,1)}, f32[4,4,64,512]{3,2,1,0:T(8,128)S(1)}) custom-call(s32[1]{0:T(128)} %bitcast.3.bit_ref, f32[7,224,512]{2,1,0:T(8,128)} %get-tuple-element.61.y2, f32[2,512]{1,0:T(2,128)S(1)} %add.309.sums2, f32[4,512]{1,0:T(4,128)S(1)} %add.312.back, ...), custom_call_target="tpu_custom_call" | custom-call | flops 3288334336 | bytes 14000000 | tf_op jit(solution)/shard_map/taps_grad_first/pallas_call | solution.py:456
  159.6 14.0 %input_grad.1 = (f32[7,224,512]{2,1,0:T(8,128)}, f32[2,512]{1,0:T(2,128)S(1)}) custom-call(s32[2]{0:T(128)S(1)} %pad_add_fusion.1.me, bf16[9,9,32,512]{3,2,1,0:T(8,128)(2,1)S(1)} %get-tuple-element.66.pad, f32[7,224,512]{2,1,0:T(8,128)} %copy-done.1, f32[2,512]{1,0:T(2,128)S(1)} %add.306.sums1, f32[4,512]{1,0:T(4,128)S(1)} %copy-done.20, ...), custom_call_target="tpu_custom_call" | custom-call | flops 7398752256 | bytes 16000000 | tf_op jit(solution)/shard_map/input_grad/pallas_call | solution.py:517
  175.6 6.5 %taps_grad_more.1 = (s16[5,272,512]{2,1,0:T(8,128)(2,1)S(1)}, f32[5,4,64,512]{3,2,1,0:T(8,128)S(1)}) custom-call(s32[1]{0:T(128)} %bitcast.3.bit_ref, bf16[9,9,32,512]{3,2,1,0:T(8,128)(2,1)S(1)} %get-tuple-element.66.pad, bf16[512,1568]{1,0:T(8,128)(2,1)S(1)} %get-tuple-element.88.turned), custom_call_target="tpu_custom_call" | custom-call | flops 4110417920 | bytes 10000000 | tf_op jit(solution)/shard_map/taps_grad_more/pallas_call | solution.py:477
  195.1 5.9 %first_grad_first.1 = (bf16[7,224,512]{2,1,0:T(8,128)(2,1)S(1)}, s16[2,272,512]{2,1,0:T(8,128)(2,1)}, f32[2,4,64,512]{3,2,1,0:T(8,128)S(1)}) custom-call(s32[1]{0:T(128)} %bitcast.3.bit_ref, f32[7,224,512]{2,1,0:T(8,128)S(1)} %copy-done.3, f32[7,224,512]{2,1,0:T(8,128)S(1)} %copy-done.2, f32[2,512]{1,0:T(2,128)S(1)} %add.306.sums1, f32[2,512]{1,0:T(2,128)S(1)} %add.315.back, ...), custom_call_target="tpu_custom_call" | custom-call | flops 1644167168 | bytes 14000000 | tf_op jit(solution)/shard_map/first_grad_first/pallas_call | solution.py:564
  202.0 2.8 copy-done
  204.8 2.9 first_grad_more.1
  218.4 5.7 %collective-permute-done.33.got = s16[2,272,512]{2,1,0:T(8,128)(2,1)S(1)} collective-permute-done((s16[2,272,512]{2,1,0:T(8,128)(2,1)S(1)}, s16[2,272,512]{2,1,0:T(8,128)(2,1)S(1)}, u32[]{:S(2)}, u32[]{:S(2)}) %collective-permute-start.33) | collective-permute-done | bytes 557088 | tf_op jit(solution)/shard_map/ppermute | solution.py:30
  228.4 7.7 %collective-permute-done.28.got = s16[2,272,512]{2,1,0:T(8,128)(2,1)S(1)} collective-permute-done((s16[2,272,512]{2,1,0:T(8,128)(2,1)}, s16[2,272,512]{2,1,0:T(8,128)(2,1)S(1)}, u32[]{:S(2)}, u32[]{:S(2)}) %collective-permute-start.28) | collective-permute-done | bytes 557088 | tf_op jit(solution)/shard_map/ppermute | solution.py:30
  255.3 5.9 %collective-permute-done.50 = s16[2,80,512]{2,1,0:T(8,128)(2,1)} collective-permute-done((s16[2,80,512]{2,1,0:T(8,128)(2,1)}, s16[2,80,512]{2,1,0:T(8,128)(2,1)}, u32[]{:S(2)}, u32[]{:S(2)}) %collective-permute-start.50) | collective-permute-done | bytes 163872 | tf_op jit(solution)/shard_map/ppermute | solution.py:30
  270.1 4.0 %add_split.14 = (s16[4,144,512]{2,1,0:T(8,128)(2,1)}, f32[4,2,64,512]{3,2,1,0:T(8,128)}) custom-call(s32[1]{0:T(128)} %bitcast.2.bit_ref, f32[4,4,64,512]{3,2,1,0:T(8,128)} %copy-done.5, s16[4,272,512]{2,1,0:T(8,128)(2,1)} %collective-permute-done.38.got), custom_call_target="tpu_custom_call" | custom-call | tf_op jit(solution)/shard_map/add_split/pallas_call | solution.py:177
  274.2 3.0 multiply_convert_fusion.4
  280.8 5.0 %add_split.16 = (s16[5,144,512]{2,1,0:T(8,128)(2,1)}, f32[5,2,64,512]{3,2,1,0:T(8,128)}) custom-call(s32[1]{0:T(128)} %bitcast.2.bit_ref, f32[5,4,64,512]{3,2,1,0:T(8,128)} %copy-done.4, s16[5,272,512]{2,1,0:T(8,128)(2,1)} %collective-permute-done.43.got), custom_call_target="tpu_custom_call" | custom-call | tf_op jit(solution)/shard_map/add_split/pallas_call | solution.py:177
  289.6 3.5 add_split.15
  298.5 12.5 %collective-permute-done.40 = s16[4,80,512]{2,1,0:T(8,128)(2,1)S(1)} collective-permute-done((s16[4,80,512]{2,1,0:T(8,128)(2,1)}, s16[4,80,512]{2,1,0:T(8,128)(2,1)S(1)}, u32[]{:S(2)}, u32[]{:S(2)}) %collective-permute-start.40) | collective-permute-done | bytes 327712 | tf_op jit(solution)/shard_map/ppermute | solution.py:30
  312.8 4.2 %add_split.17 = (s16[5,80,512]{2,1,0:T(8,128)(2,1)}, f32[5,1,64,512]{3,2,1,0:T(8,128)}) custom-call(s32[1]{0:T(128)} %bitcast.1.bit_ref, f32[5,2,64,512]{3,2,1,0:T(8,128)} %get-tuple-element.91.keep_in, s16[5,144,512]{2,1,0:T(8,128)(2,1)} %copy-done.42), custom_call_target="tpu_custom_call" | custom-call | tf_op jit(solution)/shard_map/add_split/pallas_call | solution.py:177
  317.0 3.1 collective-permute-start.45
  324.5 13.2 %collective-permute-done.45 = s16[5,80,512]{2,1,0:T(8,128)(2,1)S(1)} collective-permute-done((s16[5,80,512]{2,1,0:T(8,128)(2,1)}, s16[5,80,512]{2,1,0:T(8,128)(2,1)S(1)}, u32[]{:S(2)}, u32[]{:S(2)}) %collective-permute-start.45) | collective-permute-done | bytes 409632 | tf_op jit(solution)/shard_map/ppermute | solution.py:30
  347.1 4.8 %collective-permute-done.42 = bf16[4,64,512]{2,1,0:T(8,128)(2,1)S(1)} collective-permute-done((bf16[4,64,512]{2,1,0:T(8,128)(2,1)S(1)}, bf16[4,64,512]{2,1,0:T(8,128)(2,1)S(1)}, u32[]{:S(2)}, u32[]{:S(2)}) %collective-permute-start.42) | collective-permute-done | bytes 262176 | tf_op jit(solution)/shard_map/ppermute | solution.py:30
  352.1 6.3 %collective-permute-done.47 = bf16[5,64,512]{2,1,0:T(8,128)(2,1)S(1)} collective-permute-done((bf16[5,64,512]{2,1,0:T(8,128)(2,1)S(1)}, bf16[5,64,512]{2,1,0:T(8,128)(2,1)S(1)}, u32[]{:S(2)}, u32[]{:S(2)}) %collective-permute-start.47) | collective-permute-done | bytes 327712 | tf_op jit(solution)/shard_map/ppermute | solution.py:30
  (308 shorter events, 139.2 us)
Async XLA Ops:
  2.5 20.2 %collective-permute-start.11 = (bf16[1,11,32,512]{3,2,1,0:T(8,128)(2,1)S(1)}, bf16[1,11,32,512]{3,2,1,0:T(8,128)(2,1)S(1)}, u32[]{:S(2)}, u32[]{:S(2)}) collective-permute-start(bf16[1,11,32,512]{3,2,1,0:T(8,128)(2,1)S(1)} %maximum_bitcast_fusion.2), channel_id=1, source_target_pairs={{0,4},{1,5},{2,6},{3,7},{4,0},{5,1},{6,2},{7,3},{8,12},{9,13},{10,... | collective-permute-start | bytes 1081352 | tf_op jit(solution)/shard_map/ppermute | solution.py:30
  22.8 20.2 %collective-permute-start.12 = (bf16[2,11,32,512]{3,2,1,0:T(8,128)(2,1)S(1)}, bf16[2,11,32,512]{3,2,1,0:T(8,128)(2,1)S(1)}, u32[]{:S(2)}, u32[]{:S(2)}) collective-permute-start(bf16[2,11,32,512]{3,2,1,0:T(8,128)(2,1)S(1)} %pad_maximum_fusion.2.refs_0_), channel_id=1, source_target_pairs={{0,2},{1,3},{2,0},{3,1},{4,6},{5,7},{6,4},{7,5},{8,10},{9,11},{10,... | collective-permute-start | bytes 2162696 | tf_op jit(solution)/shard_map/ppermute | solution.py:30
  24.8 19.6 %collective-permute-start = (bf16[1,4,32,512]{3,2,1,0:T(8,128)(2,1)S(1)}, bf16[1,4,32,512]{3,2,1,0:T(8,128)(2,1)S(1)}, u32[]{:S(2)}, u32[]{:S(2)}) collective-permute-start(bf16[1,4,32,512]{3,2,1,0:T(8,128)(2,1)S(1)} %fusion.34), channel_id=1, source_target_pairs={{0,4},{1,5},{2,6},{3,7},{4,0},{5,1},{6,2},{7,3},{8,12},{9,13},{10,... | collective-permute-start | bytes 393224 | tf_op jit(solution)/shard_map/ppermute | solution.py:30
  28.2 44.9 %collective-permute-start.13 = (bf16[2,11,32,512]{3,2,1,0:T(8,128)(2,1)S(1)}, bf16[2,11,32,512]{3,2,1,0:T(8,128)(2,1)S(1)}, u32[]{:S(2)}, u32[]{:S(2)}) collective-permute-start(bf16[2,11,32,512]{3,2,1,0:T(8,128)(2,1)S(1)} %pad_maximum_fusion.2.refs_0_), channel_id=1, source_target_pairs={{0,1},{1,0},{2,3},{3,2},{4,5},{5,4},{6,7},{7,6},{8,9},{9,8},{10,11... | collective-permute-start | bytes 2162696 | tf_op jit(solution)/shard_map/ppermute | solution.py:30
  43.0 30.5 %collective-permute-start.14 = (bf16[2,11,32,512]{3,2,1,0:T(8,128)(2,1)S(1)}, bf16[2,11,32,512]{3,2,1,0:T(8,128)(2,1)S(1)}, u32[]{:S(2)}, u32[]{:S(2)}) collective-permute-start(bf16[2,11,32,512]{3,2,1,0:T(8,128)(2,1)S(1)} %collective-permute-done.12.refs_1_), channel_id=1, source_target_pairs={{0,1},{1,0},{2,3},{3,2},{4,5},{5,4},{6,7},{7,6},{8,9},{9,8},{10,11... | collective-permute-start | bytes 2162696 | tf_op jit(solution)/shard_map/ppermute | solution.py:30
  46.2 22.2 %collective-permute-start.2 = (bf16[2,4,32,512]{3,2,1,0:T(8,128)(2,1)S(1)}, bf16[2,4,32,512]{3,2,1,0:T(8,128)(2,1)}, u32[]{:S(2)}, u32[]{:S(2)}) collective-permute-start(bf16[2,4,32,512]{3,2,1,0:T(8,128)(2,1)S(1)} %pad_maximum_fusion.3.refs_0_), channel_id=1, source_target_pairs={{0,1},{1,0},{2,3},{3,2},{4,5},{5,4},{6,7},{7,6},{8,9},{9,8},{10,11... | collective-permute-start | bytes 786440 | tf_op jit(solution)/shard_map/ppermute | solution.py:30
  47.8 20.7 %collective-permute-start.4 = (bf16[2,4,32,512]{3,2,1,0:T(8,128)(2,1)S(1)}, bf16[2,4,32,512]{3,2,1,0:T(8,128)(2,1)S(1)}, u32[]{:S(2)}, u32[]{:S(2)}) collective-permute-start(bf16[2,4,32,512]{3,2,1,0:T(8,128)(2,1)S(1)} %pad_maximum_fusion.3.refs_0_), channel_id=1, source_target_pairs={{0,8},{8,0},{16,24},{24,16},{1,9},{9,1},{17,25},{25,17},{2,10},{10... | collective-permute-start | bytes 786440 | tf_op jit(solution)/shard_map/ppermute | solution.py:30
  52.2 20.3 %collective-permute-start.3 = (bf16[2,4,32,512]{3,2,1,0:T(8,128)(2,1)S(1)}, bf16[2,4,32,512]{3,2,1,0:T(8,128)(2,1)}, u32[]{:S(2)}, u32[]{:S(2)}) collective-permute-start(bf16[2,4,32,512]{3,2,1,0:T(8,128)(2,1)S(1)} %collective-permute-done.1.refs_1_), channel_id=1, source_target_pairs={{0,1},{1,0},{2,3},{3,2},{4,5},{5,4},{6,7},{7,6},{8,9},{9,8},{10,11... | collective-permute-start | bytes 786440 | tf_op jit(solution)/shard_map/ppermute | solution.py:30
  72.5 23.1 %collective-permute-start.15 = (bf16[2,11,32,512]{3,2,1,0:T(8,128)(2,1)S(1)}, bf16[2,11,32,512]{3,2,1,0:T(8,128)(2,1)S(1)}, u32[]{:S(2)}, u32[]{:S(2)}) collective-permute-start(bf16[2,11,32,512]{3,2,1,0:T(8,128)(2,1)S(1)} %pad_maximum_fusion.2.refs_0_), channel_id=1, source_target_pairs={{0,8},{8,0},{16,24},{24,16},{1,9},{9,1},{17,25},{25,17},{2,10},{10... | collective-permute-start | bytes 2162696 | tf_op jit(solution)/shard_map/ppermute | solution.py:30
  73.0 22.6 %collective-permute-start.16 = (bf16[2,11,32,512]{3,2,1,0:T(8,128)(2,1)S(1)}, bf16[2,11,32,512]{3,2,1,0:T(8,128)(2,1)S(1)}, u32[]{:S(2)}, u32[]{:S(2)}) collective-permute-start(bf16[2,11,32,512]{3,2,1,0:T(8,128)(2,1)S(1)} %collective-permute-done.12.refs_1_), channel_id=1, source_target_pairs={{0,8},{8,0},{16,24},{24,16},{1,9},{9,1},{17,25},{25,17},{2,10},{10... | collective-permute-start | bytes 2162696 | tf_op jit(solution)/shard_map/ppermute | solution.py:30
  73.1 22.6 %collective-permute-start.17 = (bf16[2,11,32,512]{3,2,1,0:T(8,128)(2,1)S(1)}, bf16[2,11,32,512]{3,2,1,0:T(8,128)(2,1)S(1)}, u32[]{:S(2)}, u32[]{:S(2)}) collective-permute-start(bf16[2,11,32,512]{3,2,1,0:T(8,128)(2,1)S(1)} %collective-permute-done.13.refs_2_), channel_id=1, source_target_pairs={{0,8},{8,0},{16,24},{24,16},{1,9},{9,1},{17,25},{25,17},{2,10},{10... | collective-permute-start | bytes 2162696 | tf_op jit(solution)/shard_map/ppermute | solution.py:30
  73.5 22.1 %collective-permute-start.18 = (bf16[2,11,32,512]{3,2,1,0:T(8,128)(2,1)S(1)}, bf16[2,11,32,512]{3,2,1,0:T(8,128)(2,1)S(1)}, u32[]{:S(2)}, u32[]{:S(2)}) collective-permute-start(bf16[2,11,32,512]{3,2,1,0:T(8,128)(2,1)S(1)} %collective-permute-done.14.refs_3_), channel_id=1, source_target_pairs={{0,8},{8,0},{16,24},{24,16},{1,9},{9,1},{17,25},{25,17},{2,10},{10... | collective-permute-start | bytes 2162696 | tf_op jit(solution)/shard_map/ppermute | solution.py:30
  138.8 76.1 %collective-permute-start.48 = (s16[2,272,512]{2,1,0:T(8,128)(2,1)}, s16[2,272,512]{2,1,0:T(8,128)(2,1)}, u32[]{:S(2)}, u32[]{:S(2)}) collective-permute-start(s16[2,272,512]{2,1,0:T(8,128)(2,1)} %pad_add_fusion), channel_id=1, source_target_pairs={{0,1},{1,0},{2,3},{3,2},{4,5},{5,4},{6,7},{7,6},{8,9},{9,8},{10,11... | collective-permute-start | bytes 1671176 | tf_op jit(solution)/shard_map/ppermute | solution.py:30
  174.1 96.0 %collective-permute-start.38 = (s16[4,272,512]{2,1,0:T(8,128)(2,1)}, s16[4,272,512]{2,1,0:T(8,128)(2,1)}, u32[]{:S(2)}, u32[]{:S(2)}) collective-permute-start(s16[4,272,512]{2,1,0:T(8,128)(2,1)} %get-tuple-element.83), channel_id=1, source_target_pairs={{0,1},{1,0},{2,3},{3,2},{4,5},{5,4},{6,7},{7,6},{8,9},{9,8},{10,11... | collective-permute-start | bytes 3342344 | tf_op jit(solution)/shard_map/ppermute | solution.py:30
  193.1 17.6 %collective-permute-start.53 = (f32[24,128]{1,0:T(8,128)S(1)}, f32[24,128]{1,0:T(8,128)S(1)}, u32[]{:S(2)}, u32[]{:S(2)}) collective-permute-start(f32[24,128]{1,0:T(8,128)S(1)} %bitcast.258), channel_id=1, source_target_pairs={{0,8},{8,0},{16,24},{24,16},{1,9},{9,1},{17,25},{25,17},{2,10},{10... | collective-permute-start | bytes 36872 | tf_op jit(solution)/shard_map/ppermute | solution.py:30
  208.7 15.4 %collective-permute-start.33 = (s16[2,272,512]{2,1,0:T(8,128)(2,1)S(1)}, s16[2,272,512]{2,1,0:T(8,128)(2,1)S(1)}, u32[]{:S(2)}, u32[]{:S(2)}) collective-permute-start(s16[2,272,512]{2,1,0:T(8,128)(2,1)S(1)} %get-tuple-element.77), channel_id=1, source_target_pairs={{0,1},{1,0},{2,3},{3,2},{4,5},{5,4},{6,7},{7,6},{8,9},{9,8},{10,11... | collective-permute-start | bytes 1671176 | tf_op jit(solution)/shard_map/ppermute | solution.py:30
  209.2 26.9 %collective-permute-start.28 = (s16[2,272,512]{2,1,0:T(8,128)(2,1)}, s16[2,272,512]{2,1,0:T(8,128)(2,1)S(1)}, u32[]{:S(2)}, u32[]{:S(2)}) collective-permute-start(s16[2,272,512]{2,1,0:T(8,128)(2,1)} %get-tuple-element.70), channel_id=1, source_target_pairs={{0,1},{1,0},{2,3},{3,2},{4,5},{5,4},{6,7},{7,6},{8,9},{9,8},{10,11... | collective-permute-start | bytes 1671176 | tf_op jit(solution)/shard_map/ppermute | solution.py:30
  214.4 66.4 %collective-permute-start.43 = (s16[5,272,512]{2,1,0:T(8,128)(2,1)S(1)}, s16[5,272,512]{2,1,0:T(8,128)(2,1)}, u32[]{:S(2)}, u32[]{:S(2)}) collective-permute-start(s16[5,272,512]{2,1,0:T(8,128)(2,1)S(1)} %copy-done.22), channel_id=1, source_target_pairs={{0,1},{1,0},{2,3},{3,2},{4,5},{5,4},{6,7},{7,6},{8,9},{9,8},{10,11... | collective-permute-start | bytes 4177928 | tf_op jit(solution)/shard_map/ppermute | solution.py:30
  217.2 23.7 %collective-permute-start.49 = (s16[2,144,512]{2,1,0:T(8,128)(2,1)}, s16[2,144,512]{2,1,0:T(8,128)(2,1)S(1)}, u32[]{:S(2)}, u32[]{:S(2)}) collective-permute-start(s16[2,144,512]{2,1,0:T(8,128)(2,1)} %get-tuple-element.97), channel_id=1, source_target_pairs={{0,2},{1,3},{2,0},{3,1},{4,6},{5,7},{6,4},{7,5},{8,10},{9,11},{10,... | collective-permute-start | bytes 884744 | tf_op jit(solution)/shard_map/ppermute | solution.py:30
  227.2 19.7 %collective-permute-start.34 = (s16[2,144,512]{2,1,0:T(8,128)(2,1)}, s16[2,144,512]{2,1,0:T(8,128)(2,1)S(1)}, u32[]{:S(2)}, u32[]{:S(2)}) collective-permute-start(s16[2,144,512]{2,1,0:T(8,128)(2,1)} %get-tuple-element.79), channel_id=1, source_target_pairs={{0,2},{1,3},{2,0},{3,1},{4,6},{5,7},{6,4},{7,5},{8,10},{9,11},{10,... | collective-permute-start | bytes 884744 | tf_op jit(solution)/shard_map/ppermute | solution.py:30
  243.6 17.7 %collective-permute-start.50 = (s16[2,80,512]{2,1,0:T(8,128)(2,1)}, s16[2,80,512]{2,1,0:T(8,128)(2,1)}, u32[]{:S(2)}, u32[]{:S(2)}) collective-permute-start(s16[2,80,512]{2,1,0:T(8,128)(2,1)} %get-tuple-element.99), channel_id=1, source_target_pairs={{0,4},{1,5},{2,6},{3,7},{4,0},{5,1},{6,2},{7,3},{8,12},{9,13},{10,... | collective-permute-start | bytes 491528 | tf_op jit(solution)/shard_map/ppermute | solution.py:30
  249.6 15.6 %collective-permute-start.35 = (s16[2,80,512]{2,1,0:T(8,128)(2,1)}, s16[2,80,512]{2,1,0:T(8,128)(2,1)S(1)}, u32[]{:S(2)}, u32[]{:S(2)}) collective-permute-start(s16[2,80,512]{2,1,0:T(8,128)(2,1)} %get-tuple-element.81), channel_id=1, source_target_pairs={{0,4},{1,5},{2,6},{3,7},{4,0},{5,1},{6,2},{7,3},{8,12},{9,13},{10,... | collective-permute-start | bytes 491528 | tf_op jit(solution)/shard_map/ppermute | solution.py:30
  252.7 14.9 %collective-permute-start.30 = (s16[2,80,512]{2,1,0:T(8,128)(2,1)}, s16[2,80,512]{2,1,0:T(8,128)(2,1)S(1)}, u32[]{:S(2)}, u32[]{:S(2)}) collective-permute-start(s16[2,80,512]{2,1,0:T(8,128)(2,1)} %get-tuple-element.74), channel_id=1, source_target_pairs={{0,4},{1,5},{2,6},{3,7},{4,0},{5,1},{6,2},{7,3},{8,12},{9,13},{10,... | collective-permute-start | bytes 491528 | tf_op jit(solution)/shard_map/ppermute | solution.py:30
  274.2 15.4 %collective-permute-start.39 = (s16[4,144,512]{2,1,0:T(8,128)(2,1)}, s16[4,144,512]{2,1,0:T(8,128)(2,1)}, u32[]{:S(2)}, u32[]{:S(2)}) collective-permute-start(s16[4,144,512]{2,1,0:T(8,128)(2,1)} %get-tuple-element.85), channel_id=1, source_target_pairs={{0,2},{1,3},{2,0},{3,1},{4,6},{5,7},{6,4},{7,5},{8,10},{9,11},{10,... | collective-permute-start | bytes 1769480 | tf_op jit(solution)/shard_map/ppermute | solution.py:30
  277.2 16.8 %collective-permute-start.31 = (bf16[2,64,512]{2,1,0:T(8,128)(2,1)S(1)}, bf16[2,64,512]{2,1,0:T(8,128)(2,1)}, u32[]{:S(2)}, u32[]{:S(2)}) collective-permute-start(bf16[2,64,512]{2,1,0:T(8,128)(2,1)S(1)} %get-tuple-element.123), channel_id=1, source_target_pairs={{0,8},{8,0},{16,24},{24,16},{1,9},{9,1},{17,25},{25,17},{2,10},{10... | collective-permute-start | bytes 393224 | tf_op jit(solution)/shard_map/ppermute | solution.py:30
  279.4 17.1 %collective-permute-start.52 = (bf16[64,1000]{1,0:T(8,128)(2,1)}, bf16[64,1000]{1,0:T(8,128)(2,1)}, u32[]{:S(2)}, u32[]{:S(2)}) collective-permute-start(bf16[64,1000]{1,0:T(8,128)(2,1)} %add_convert_fusion.2), channel_id=1, source_target_pairs={{0,16},{8,24},{16,0},{24,8},{1,17},{9,25},{17,1},{25,9},{2,18},{10... | collective-permute-start | bytes 384008 | tf_op jit(solution)/shard_map/ppermute | solution.py:30
  285.9 26.0 %collective-permute-start.44 = (s16[5,144,512]{2,1,0:T(8,128)(2,1)}, s16[5,144,512]{2,1,0:T(8,128)(2,1)S(1)}, u32[]{:S(2)}, u32[]{:S(2)}) collective-permute-start(s16[5,144,512]{2,1,0:T(8,128)(2,1)} %get-tuple-element.92), channel_id=1, source_target_pairs={{0,2},{1,3},{2,0},{3,1},{4,6},{5,7},{6,4},{7,5},{8,10},{9,11},{10,... | collective-permute-start | bytes 2211848 | tf_op jit(solution)/shard_map/ppermute | solution.py:30
  289.0 52.4 %collective-permute-start.37 = (bf16[2,64,512]{2,1,0:T(8,128)(2,1)S(1)}, bf16[2,64,512]{2,1,0:T(8,128)(2,1)}, u32[]{:S(2)}, u32[]{:S(2)}) collective-permute-start(bf16[2,64,512]{2,1,0:T(8,128)(2,1)S(1)} %add_convert_fusion.3), channel_id=1, source_target_pairs={{0,16},{8,24},{16,0},{24,8},{1,17},{9,25},{17,1},{25,9},{2,18},{10... | collective-permute-start | bytes 393224 | tf_op jit(solution)/shard_map/ppermute | solution.py:30
  293.1 17.9 %collective-permute-start.40 = (s16[4,80,512]{2,1,0:T(8,128)(2,1)}, s16[4,80,512]{2,1,0:T(8,128)(2,1)S(1)}, u32[]{:S(2)}, u32[]{:S(2)}) collective-permute-start(s16[4,80,512]{2,1,0:T(8,128)(2,1)} %get-tuple-element.87), channel_id=1, source_target_pairs={{0,4},{1,5},{2,6},{3,7},{4,0},{5,1},{6,2},{7,3},{8,12},{9,13},{10,... | collective-permute-start | bytes 983048 | tf_op jit(solution)/shard_map/ppermute | solution.py:30
  294.9 46.4 %collective-permute-start.32 = (bf16[2,64,512]{2,1,0:T(8,128)(2,1)S(1)}, bf16[2,64,512]{2,1,0:T(8,128)(2,1)}, u32[]{:S(2)}, u32[]{:S(2)}) collective-permute-start(bf16[2,64,512]{2,1,0:T(8,128)(2,1)S(1)} %add_convert_fusion.4), channel_id=1, source_target_pairs={{0,16},{8,24},{16,0},{24,8},{1,17},{9,25},{17,1},{25,9},{2,18},{10... | collective-permute-start | bytes 393224 | tf_op jit(solution)/shard_map/ppermute | solution.py:30
  317.0 20.8 %collective-permute-start.45 = (s16[5,80,512]{2,1,0:T(8,128)(2,1)}, s16[5,80,512]{2,1,0:T(8,128)(2,1)S(1)}, u32[]{:S(2)}, u32[]{:S(2)}) collective-permute-start(s16[5,80,512]{2,1,0:T(8,128)(2,1)} %get-tuple-element.94), channel_id=1, source_target_pairs={{0,4},{1,5},{2,6},{3,7},{4,0},{5,1},{6,2},{7,3},{8,12},{9,13},{10,... | collective-permute-start | bytes 1228808 | tf_op jit(solution)/shard_map/ppermute | solution.py:30
  324.4 18.2 %collective-permute-start.41 = (bf16[4,64,512]{2,1,0:T(8,128)(2,1)S(1)}, bf16[4,64,512]{2,1,0:T(8,128)(2,1)S(1)}, u32[]{:S(2)}, u32[]{:S(2)}) collective-permute-start(bf16[4,64,512]{2,1,0:T(8,128)(2,1)S(1)} %get-tuple-element.130), channel_id=1, source_target_pairs={{0,8},{8,0},{16,24},{24,16},{1,9},{9,1},{17,25},{25,17},{2,10},{10... | collective-permute-start | bytes 786440 | tf_op jit(solution)/shard_map/ppermute | solution.py:30
  (88 other events, 691.8 us)
